TPU v7x, 512 devices: a whole 4x4x16 slice. The times are simulated.
512 devices in a mesh: blk: 64 (over z, x_lo, core), grp: 8 (over y, x_hi).
Axes of the slice: x: 4 (x_hi: 2, x_lo: 2; x = x_hi * 2 + x_lo), y: 4, z: 16, core: 2. Of those that a mesh axis runs over, the one named last changes fastest.
Arguments:
- view_one: float32 [131072, 256], P(('blk', 'grp')), may hold values from -4 to 4
- view_two: float32 [131072, 256], P(('blk', 'grp')), may hold values from -4 to 4
- node_ids: int32 [131072], P(('blk', 'grp')), may hold values from 0 to 2999999
Outputs:
- grad_one: float32 [131072, 256], P(('blk', 'grp'))
- grad_two: float32 [131072, 256], P(('blk', 'grp'))
Inputs may be any that keep to these rules, and one draw needn't show every extreme that they name: `node_ids`: some ids repeat within the batch.
All inputs are finite; a program needn't handle non-finite values.
Results may differ from a plain program's by a relative error of at most 0.0003.
Values sent between devices are 32-bit elements; how exact they have to be, the bound alone decides.
A program may use at most 64 MiB of HBM per device.

v0:
```python
import jax
import jax.numpy as jnp
from jax import lax
from jax.sharding import PartitionSpec as P

ROUNDS = 5


logit_sharpness_divisor = 0.5


def from_partner(x, axis, distance):
    return lax.ppermute(x, axis, [(i, i ^ 1 << distance) for i in range(lax.axis_size(axis))])


def unit_rows(z):
    radius = jnp.sqrt(jnp.sum(z * z, axis=1, keepdims=True) + 1e-06)
    return (z / radius, radius)


def scored(a, b):
    return jnp.dot(a, b.T, precision=lax.Precision.HIGHEST, preferred_element_type=jnp.float32)


def applied(a, b):
    return jnp.dot(a, b, precision=lax.Precision.HIGHEST, preferred_element_type=jnp.float32)


def exps(cosine_logit_matrix, retained_pair_filter):
    return jnp.where(
        retained_pair_filter, jnp.exp(cosine_logit_matrix / logit_sharpness_divisor), 0.0
    )


def differ(left, right):
    return (left[0][:, None] != right[0][None, :]) | (left[1][:, None] != right[1][None, :])


def trade_views(stacked, id_pair, bit):
    return from_partner((stacked, id_pair), ("blk", "grp"), bit)


def trade_dens(dens, bit):
    return from_partner(dens, ("blk", "grp"), bit)


def on_device(view_one, view_two, node_ids):
    rows = view_one.shape[0]
    anchor_node_vectors, radius_one = unit_rows(view_one)
    partnered_node_vectors, radius_two = unit_rows(view_two)
    id_pair = jnp.stack([node_ids // 65536, node_ids % 65536]).astype(jnp.float32)
    stacked = jnp.stack([anchor_node_vectors, partnered_node_vectors])
    own_same = differ(id_pair, id_pair)
    own_cross = own_same | jnp.eye(rows, dtype=bool)
    own_uv = exps(scored(anchor_node_vectors, partnered_node_vectors), own_cross)
    own_uu = exps(scored(anchor_node_vectors, anchor_node_vectors), own_same)
    own_vu = exps(scored(partnered_node_vectors, anchor_node_vectors), own_cross)
    own_vv = exps(scored(partnered_node_vectors, partnered_node_vectors), own_same)
    den_u = jnp.sum(own_uv, axis=1) + jnp.sum(own_uu, axis=1)
    den_v = jnp.sum(own_vu, axis=1) + jnp.sum(own_vv, axis=1)
    stored = []
    for bit in range(ROUNDS):
        partner, partner_ids = trade_views(stacked, id_pair, bit)
        retained_pair_filter = differ(id_pair, partner_ids)
        pu, pv = (partner[0], partner[1])
        blocks = (
            exps(scored(anchor_node_vectors, pv), retained_pair_filter),
            exps(scored(anchor_node_vectors, pu), retained_pair_filter),
            exps(scored(partnered_node_vectors, pu), retained_pair_filter),
            exps(scored(partnered_node_vectors, pv), retained_pair_filter),
        )
        den_u = den_u + jnp.sum(blocks[0], axis=1) + jnp.sum(blocks[1], axis=1)
        den_v = den_v + jnp.sum(blocks[2], axis=1) + jnp.sum(blocks[3], axis=1)
        stored.append((pu, pv, blocks))
    inv_u = 1.0 / den_u
    inv_v = 1.0 / den_v
    dens = jnp.stack([den_u, den_v])
    anchor_node_derivative = applied(
        own_uv * (inv_u[:, None] + inv_v[None, :]), partnered_node_vectors
    ) + applied(own_uu * (inv_u[:, None] + inv_u[None, :]), anchor_node_vectors)
    partnered_node_derivative = applied(
        own_vu * (inv_v[:, None] + inv_u[None, :]), anchor_node_vectors
    ) + applied(own_vv * (inv_v[:, None] + inv_v[None, :]), partnered_node_vectors)
    for bit in range(ROUNDS):
        pu, pv, blocks = stored[bit]
        partner_inv = 1.0 / trade_dens(dens, bit)
        anchor_node_derivative = anchor_node_derivative + applied(
            blocks[0] * (inv_u[:, None] + partner_inv[1][None, :]), pv
        )
        anchor_node_derivative = anchor_node_derivative + applied(
            blocks[1] * (inv_u[:, None] + partner_inv[0][None, :]), pu
        )
        partnered_node_derivative = partnered_node_derivative + applied(
            blocks[2] * (inv_v[:, None] + partner_inv[0][None, :]), pu
        )
        partnered_node_derivative = partnered_node_derivative + applied(
            blocks[3] * (inv_v[:, None] + partner_inv[1][None, :]), pv
        )
    anchor_node_derivative = (
        anchor_node_derivative / (2.0 * logit_sharpness_divisor)
        - partnered_node_vectors / logit_sharpness_divisor
    )
    partnered_node_derivative = (
        partnered_node_derivative / (2.0 * logit_sharpness_divisor)
        - anchor_node_vectors / logit_sharpness_divisor
    )
    grad_one = (
        anchor_node_derivative / radius_one
        - view_one
        * jnp.sum(view_one * anchor_node_derivative, axis=1, keepdims=True)
        / radius_one**3
    )
    grad_two = (
        partnered_node_derivative / radius_two
        - view_two
        * jnp.sum(view_two * partnered_node_derivative, axis=1, keepdims=True)
        / radius_two**3
    )
    return (grad_one, grad_two)


def solution(mesh):
    placed = (P(("blk", "grp"), None), P(("blk", "grp"), None), P(("blk", "grp")))
    return jax.shard_map(
        on_device,
        mesh=mesh,
        in_specs=placed,
        out_specs=(P(("blk", "grp"), None), P(("blk", "grp"), None)),
        check_vma=False,
    )
```

profile of v0, /device:TPU:6, one launch (start us, length us, event | category | flops | bytes accessed | tf_op | source)
XLA Modules:
  0.0 107.5 jit_solution(8782159909479633833)
XLA Ops:
  1.4 1.9 %collective-permute-start.6 = (f32[2,256]{1,0:T(2,128)S(1)}, f32[2,256]{1,0:T(2,128)S(1)}, u32[]{:S(2)}, u32[]{:S(2)}) collective-permute-start(f32[2,256]{1,0:T(2,128)S(1)} %add_convert_fusion), channel_id=1, source_target_pairs={{0,8},{1,9},{2,10},{3,11},{4,12},{5,13},{6,14},{7,15},{8,0},{9,1},... | collective-permute-start | bytes 6152 | tf_op jit(solution)/shard_map/ppermute | solution.py:13
  3.3 5.1 %collective-permute-start.4 = (f32[2,256]{1,0:T(2,128)S(1)}, f32[2,256]{1,0:T(2,128)S(1)}, u32[]{:S(2)}, u32[]{:S(2)}) collective-permute-start(f32[2,256]{1,0:T(2,128)S(1)} %add_convert_fusion), channel_id=1, source_target_pairs={{0,4},{1,5},{2,6},{3,7},{4,0},{5,1},{6,2},{7,3},{8,12},{9,13},{10,... | collective-permute-start | bytes 6152 | tf_op jit(solution)/shard_map/ppermute | solution.py:13
  8.4 2.6 %collective-permute-start.2 = (f32[2,256]{1,0:T(2,128)S(1)}, f32[2,256]{1,0:T(2,128)S(1)}, u32[]{:S(2)}, u32[]{:S(2)}) collective-permute-start(f32[2,256]{1,0:T(2,128)S(1)} %add_convert_fusion), channel_id=1, source_target_pairs={{0,2},{1,3},{2,0},{3,1},{4,6},{5,7},{6,4},{7,5},{8,10},{9,11},{10,... | collective-permute-start | bytes 6152 | tf_op jit(solution)/shard_map/ppermute | solution.py:13
  11.0 3.3 %collective-permute-start = (f32[2,256]{1,0:T(2,128)S(1)}, f32[2,256]{1,0:T(2,128)S(1)}, u32[]{:S(2)}, u32[]{:S(2)}) collective-permute-start(f32[2,256]{1,0:T(2,128)S(1)} %add_convert_fusion), channel_id=1, source_target_pairs={{0,1},{1,0},{2,3},{3,2},{4,5},{5,4},{6,7},{7,6},{8,9},{9,8},{10,11... | collective-permute-start | bytes 6152 | tf_op jit(solution)/shard_map/ppermute | solution.py:13
  14.3 3.4 %collective-permute-start.8 = (f32[2,256]{1,0:T(2,128)S(1)}, f32[2,256]{1,0:T(2,128)S(1)}, u32[]{:S(2)}, u32[]{:S(2)}) collective-permute-start(f32[2,256]{1,0:T(2,128)S(1)} %add_convert_fusion), channel_id=1, source_target_pairs={{0,16},{1,17},{2,18},{3,19},{4,20},{5,21},{6,22},{7,23},{8,24},{9,... | collective-permute-start | bytes 6152 | tf_op jit(solution)/shard_map/ppermute | solution.py:13
  17.7 1.1 multiply_reduce_fusion.3
  22.7 2.5 %collective-permute-start.9 = (f32[2,256,256]{1,2,0:T(8,128)S(1)}, f32[2,256,256]{1,2,0:T(8,128)S(1)}, u32[]{:S(2)}, u32[]{:S(2)}) collective-permute-start(f32[2,256,256]{1,2,0:T(8,128)S(1)} %pad_maximum_fusion), channel_id=1, source_target_pairs={{0,16},{1,17},{2,18},{3,19},{4,20},{5,21},{6,22},{7,23},{8,24},{9,... | collective-permute-start | bytes 1572872 | tf_op jit(solution)/shard_map/ppermute | solution.py:13
  25.2 1.9 %collective-permute-start.7 = (f32[2,256,256]{1,2,0:T(8,128)S(1)}, f32[2,256,256]{1,2,0:T(8,128)S(1)}, u32[]{:S(2)}, u32[]{:S(2)}) collective-permute-start(f32[2,256,256]{1,2,0:T(8,128)S(1)} %pad_maximum_fusion), channel_id=1, source_target_pairs={{0,8},{1,9},{2,10},{3,11},{4,12},{5,13},{6,14},{7,15},{8,0},{9,1},... | collective-permute-start | bytes 1572872 | tf_op jit(solution)/shard_map/ppermute | solution.py:13
  27.1 4.9 %collective-permute-start.5 = (f32[2,256,256]{1,2,0:T(8,128)S(1)}, f32[2,256,256]{1,2,0:T(8,128)S(1)}, u32[]{:S(2)}, u32[]{:S(2)}) collective-permute-start(f32[2,256,256]{1,2,0:T(8,128)S(1)} %pad_maximum_fusion), channel_id=1, source_target_pairs={{0,4},{1,5},{2,6},{3,7},{4,0},{5,1},{6,2},{7,3},{8,12},{9,13},{10,... | collective-permute-start | bytes 1572872 | tf_op jit(solution)/shard_map/ppermute | solution.py:13
  32.0 3.3 %collective-permute-start.3 = (f32[2,256,256]{1,2,0:T(8,128)S(1)}, f32[2,256,256]{1,2,0:T(8,128)S(1)}, u32[]{:S(2)}, u32[]{:S(2)}) collective-permute-start(f32[2,256,256]{1,2,0:T(8,128)S(1)} %pad_maximum_fusion), channel_id=1, source_target_pairs={{0,2},{1,3},{2,0},{3,1},{4,6},{5,7},{6,4},{7,5},{8,10},{9,11},{10,... | collective-permute-start | bytes 1572872 | tf_op jit(solution)/shard_map/ppermute | solution.py:13
  35.4 2.7 %collective-permute-start.1 = (f32[2,256,256]{1,2,0:T(8,128)S(1)}, f32[2,256,256]{1,2,0:T(8,128)S(1)}, u32[]{:S(2)}, u32[]{:S(2)}) collective-permute-start(f32[2,256,256]{1,2,0:T(8,128)S(1)} %pad_maximum_fusion), channel_id=1, source_target_pairs={{0,1},{1,0},{2,3},{3,2},{4,5},{5,4},{6,7},{7,6},{8,9},{9,8},{10,11... | collective-permute-start | bytes 1572872 | tf_op jit(solution)/shard_map/ppermute | solution.py:13
  40.9 4.4 %collective-permute-done.5 = f32[2,256,256]{1,2,0:T(8,128)S(1)} collective-permute-done((f32[2,256,256]{1,2,0:T(8,128)S(1)}, f32[2,256,256]{1,2,0:T(8,128)S(1)}, u32[]{:S(2)}, u32[]{:S(2)}) %collective-permute-start.5) | collective-permute-done | bytes 524320 | tf_op jit(solution)/shard_map/ppermute | solution.py:13
  46.5 10.4 %collective-permute-done.3 = f32[2,256,256]{1,2,0:T(8,128)S(1)} collective-permute-done((f32[2,256,256]{1,2,0:T(8,128)S(1)}, f32[2,256,256]{1,2,0:T(8,128)S(1)}, u32[]{:S(2)}, u32[]{:S(2)}) %collective-permute-start.3) | collective-permute-done | bytes 524320 | tf_op jit(solution)/shard_map/ppermute | solution.py:13
  59.5 1.3 %fusion.210 = (f32[256]{0:T(256)S(1)}, f32[256,256]{0,1:T(8,128)}) fusion(f32[2,256,256]{1,2,0:T(8,128)S(1)} %collective-permute-done.9, f32[256,256]{0,1:T(8,128)S(1)} %copy.5, f32[256]{0:T(256)S(1)} %get-tuple-element.33, f32[256]{0:T(256)S(1)} %bitcast.244, f32[256]{0:T(256)S(1)} %bitcast.196, f32[256]{0:T(256)S(1)} %bitcast.240, f32[256]{0:T(256)S(1)} %bitcast.172), kind=kOutput, calls=%fused_computation.286 | convolution fusion | flops 201785088 | bytes 792576 | tf_op jit(solution)/shard_map/dot_general | solution.py:22
  60.8 1.3 %fusion.211 = (f32[256]{0:T(256)S(1)}, f32[256,256]{0,1:T(8,128)}) fusion(f32[2,256,256]{1,2,0:T(8,128)S(1)} %collective-permute-done.9, f32[256,256]{0,1:T(8,128)S(1)} %copy.5, f32[256]{0:T(256)S(1)} %get-tuple-element.33, f32[256]{0:T(256)S(1)} %bitcast.245, f32[256]{0:T(256)S(1)} %bitcast.197, f32[256]{0:T(256)S(1)} %bitcast.241, f32[256]{0:T(256)S(1)} %bitcast.173), kind=kOutput, calls=%fused_computation.287 | convolution fusion | flops 201785088 | bytes 792576 | tf_op jit(solution)/shard_map/dot_general | solution.py:22
  62.1 1.3 %fusion.212 = (f32[256]{0:T(256)S(1)}, f32[256,256]{0,1:T(8,128)}) fusion(f32[2,256,256]{1,2,0:T(8,128)S(1)} %collective-permute-done.7, f32[256,256]{0,1:T(8,128)S(1)} %copy.5, f32[256]{0:T(256)S(1)} %get-tuple-element.33, f32[256]{0:T(256)S(1)} %bitcast.212, f32[256]{0:T(256)S(1)} %bitcast.198, f32[256]{0:T(256)S(1)} %bitcast.208, f32[256]{0:T(256)S(1)} %bitcast.174), kind=kOutput, calls=%fused_computation.288 | convolution fusion | flops 201785088 | bytes 792576 | tf_op jit(solution)/shard_map/dot_general | solution.py:22
  63.4 1.3 %fusion.213 = (f32[256]{0:T(256)S(1)}, f32[256,256]{0,1:T(8,128)}) fusion(f32[2,256,256]{1,2,0:T(8,128)S(1)} %collective-permute-done.7, f32[256,256]{0,1:T(8,128)S(1)} %copy.5, f32[256]{0:T(256)S(1)} %get-tuple-element.33, f32[256]{0:T(256)S(1)} %bitcast.213, f32[256]{0:T(256)S(1)} %bitcast.199, f32[256]{0:T(256)S(1)} %bitcast.209, f32[256]{0:T(256)S(1)} %bitcast.175), kind=kOutput, calls=%fused_computation.289 | convolution fusion | flops 201785088 | bytes 792576 | tf_op jit(solution)/shard_map/dot_general | solution.py:22
  64.7 1.3 %fusion.214 = (f32[256]{0:T(256)S(1)}, f32[256,256]{0,1:T(8,128)}) fusion(f32[2,256,256]{1,2,0:T(8,128)S(1)} %collective-permute-done.5, f32[256,256]{0,1:T(8,128)S(1)} %copy.5, f32[256]{0:T(256)S(1)} %get-tuple-element.33, f32[256]{0:T(256)S(1)} %bitcast.220, f32[256]{0:T(256)S(1)} %bitcast.200, f32[256]{0:T(256)S(1)} %bitcast.216, f32[256]{0:T(256)S(1)} %bitcast.176), kind=kOutput, calls=%fused_computation.290 | convolution fusion | flops 201785088 | bytes 792576 | tf_op jit(solution)/shard_map/dot_general | solution.py:22
  66.1 1.3 %fusion.215 = (f32[256]{0:T(256)S(1)}, f32[256,256]{0,1:T(8,128)}) fusion(f32[2,256,256]{1,2,0:T(8,128)S(1)} %collective-permute-done.5, f32[256,256]{0,1:T(8,128)S(1)} %copy.5, f32[256]{0:T(256)S(1)} %get-tuple-element.33, f32[256]{0:T(256)S(1)} %bitcast.221, f32[256]{0:T(256)S(1)} %bitcast.201, f32[256]{0:T(256)S(1)} %bitcast.217, f32[256]{0:T(256)S(1)} %bitcast.177), kind=kOutput, calls=%fused_computation.291 | convolution fusion | flops 201785088 | bytes 792576 | tf_op jit(solution)/shard_map/dot_general | solution.py:22
  67.4 1.3 %fusion.216 = (f32[256]{0:T(256)S(1)}, f32[256,256]{0,1:T(8,128)}) fusion(f32[2,256,256]{1,2,0:T(8,128)S(1)} %collective-permute-done.3, f32[256,256]{0,1:T(8,128)S(1)} %copy.5, f32[256]{0:T(256)S(1)} %get-tuple-element.33, f32[256]{0:T(256)S(1)} %bitcast.228, f32[256]{0:T(256)S(1)} %bitcast.202, f32[256]{0:T(256)S(1)} %bitcast.224, f32[256]{0:T(256)S(1)} %bitcast.178), kind=kOutput, calls=%fused_computation.292 | convolution fusion | flops 201785088 | bytes 792576 | tf_op jit(solution)/shard_map/dot_general | solution.py:22
  68.7 1.3 %fusion.217 = (f32[256]{0:T(256)S(1)}, f32[256,256]{0,1:T(8,128)}) fusion(f32[2,256,256]{1,2,0:T(8,128)S(1)} %collective-permute-done.3, f32[256,256]{0,1:T(8,128)S(1)} %copy.5, f32[256]{0:T(256)S(1)} %get-tuple-element.33, f32[256]{0:T(256)S(1)} %bitcast.229, f32[256]{0:T(256)S(1)} %bitcast.203, f32[256]{0:T(256)S(1)} %bitcast.225, f32[256]{0:T(256)S(1)} %bitcast.179), kind=kOutput, calls=%fused_computation.293 | convolution fusion | flops 201785088 | bytes 792576 | tf_op jit(solution)/shard_map/dot_general | solution.py:22
  70.1 1.3 %fusion.218 = (f32[256]{0:T(256)S(1)}, f32[256,256]{0,1:T(8,128)}) fusion(f32[2,256,256]{1,2,0:T(8,128)S(1)} %collective-permute-done.1, f32[256,256]{0,1:T(8,128)S(1)} %copy.5, f32[256]{0:T(256)S(1)} %get-tuple-element.33, f32[256]{0:T(256)S(1)} %bitcast.236, f32[256]{0:T(256)S(1)} %bitcast.204, f32[256]{0:T(256)S(1)} %bitcast.232, f32[256]{0:T(256)S(1)} %bitcast.180), kind=kOutput, calls=%fused_computation.294 | convolution fusion | flops 201785088 | bytes 792576 | tf_op jit(solution)/shard_map/dot_general | solution.py:22
  71.4 1.6 %fusion.219 = (f32[256]{0:T(256)S(1)}, f32[256,256]{0,1:T(8,128)}) fusion(f32[2,256,256]{1,2,0:T(8,128)S(1)} %collective-permute-done.1, f32[256,256]{0,1:T(8,128)S(1)} %copy.5, f32[256]{0:T(256)S(1)} %get-tuple-element.33, f32[256]{0:T(256)S(1)} %bitcast.237, f32[256]{0:T(256)S(1)} %bitcast.205, f32[256]{0:T(256)S(1)} %bitcast.233, f32[256]{0:T(256)S(1)} %bitcast.181), kind=kOutput, calls=%fused_computation.295 | convolution fusion | flops 201785088 | bytes 792576 | tf_op jit(solution)/shard_map/dot_general | solution.py:22
  73.0 3.9 %collective-permute-start.14 = (f32[2,256]{1,0:T(2,128)S(1)}, f32[2,256]{1,0:T(2,128)S(1)}, u32[]{:S(2)}, u32[]{:S(2)}) collective-permute-start(f32[2,256]{1,0:T(2,128)S(1)} %pad_maximum_fusion.1), channel_id=1, source_target_pairs={{0,16},{1,17},{2,18},{3,19},{4,20},{5,21},{6,22},{7,23},{8,24},{9,... | collective-permute-start | bytes 6152 | tf_op jit(solution)/shard_map/ppermute | solution.py:13
  76.9 1.9 %collective-permute-start.13 = (f32[2,256]{1,0:T(2,128)S(1)}, f32[2,256]{1,0:T(2,128)S(1)}, u32[]{:S(2)}, u32[]{:S(2)}) collective-permute-start(f32[2,256]{1,0:T(2,128)S(1)} %pad_maximum_fusion.1), channel_id=1, source_target_pairs={{0,8},{1,9},{2,10},{3,11},{4,12},{5,13},{6,14},{7,15},{8,0},{9,1},... | collective-permute-start | bytes 6152 | tf_op jit(solution)/shard_map/ppermute | solution.py:13
  78.8 3.1 %collective-permute-start.12 = (f32[2,256]{1,0:T(2,128)S(1)}, f32[2,256]{1,0:T(2,128)S(1)}, u32[]{:S(2)}, u32[]{:S(2)}) collective-permute-start(f32[2,256]{1,0:T(2,128)S(1)} %pad_maximum_fusion.1), channel_id=1, source_target_pairs={{0,4},{1,5},{2,6},{3,7},{4,0},{5,1},{6,2},{7,3},{8,12},{9,13},{10,... | collective-permute-start | bytes 6152 | tf_op jit(solution)/shard_map/ppermute | solution.py:13
  82.0 1.9 %collective-permute-start.11 = (f32[2,256]{1,0:T(2,128)S(1)}, f32[2,256]{1,0:T(2,128)S(1)}, u32[]{:S(2)}, u32[]{:S(2)}) collective-permute-start(f32[2,256]{1,0:T(2,128)S(1)} %pad_maximum_fusion.1), channel_id=1, source_target_pairs={{0,2},{1,3},{2,0},{3,1},{4,6},{5,7},{6,4},{7,5},{8,10},{9,11},{10,... | collective-permute-start | bytes 6152 | tf_op jit(solution)/shard_map/ppermute | solution.py:13
  83.9 3.3 %collective-permute-start.10 = (f32[2,256]{1,0:T(2,128)S(1)}, f32[2,256]{1,0:T(2,128)S(1)}, u32[]{:S(2)}, u32[]{:S(2)}) collective-permute-start(f32[2,256]{1,0:T(2,128)S(1)} %pad_maximum_fusion.1), channel_id=1, source_target_pairs={{0,1},{1,0},{2,3},{3,2},{4,5},{5,4},{6,7},{7,6},{8,9},{9,8},{10,11... | collective-permute-start | bytes 6152 | tf_op jit(solution)/shard_map/ppermute | solution.py:13
  88.7 1.2 %convolution_add_fusion.3 = f32[256,256]{0,1:T(8,128)} fusion(f32[256,256]{0,1:T(8,128)S(1)} %fusion.133, f32[256,256]{0,1:T(8,128)S(1)} %get-tuple-element.83, f32[256]{0:T(256)S(1)} %get-tuple-element.6, f32[256,256]{0,1:T(8,128)S(1)} %copy.5, f32[256]{0:T(256)S(1)} %get-tuple-element.33), kind=kOutput, calls=%fused_computation.5 | convolution fusion | flops 201588736 | bytes 1050624 | tf_op jit(solution)/shard_map/dot_general | solution.py:26
  90.0 0.8 collective-permute-done.10
  96.0 0.8 copy.12
  96.8 1.5 %fusion.102 = f32[256,256]{0,1:T(8,128)S(1)} fusion(f32[256,256]{0,1:T(8,128)} %get-tuple-element.61, f32[2,256,256]{1,2,0:T(8,128)S(1)} %collective-permute-done.9, f32[256]{0:T(256)S(1)} %bitcast.145, f32[256]{0:T(256)S(1)} %get-tuple-element.6), kind=kOutput, calls=%fused_computation.145 | convolution fusion | flops 201457664 | bytes 788480 | tf_op jit(solution)/shard_map/dot_general | solution.py:26
  (103 shorter events, 26.7 us)
Async XLA Ops:
  0.6 18.2 %copy-start = (f32[256,256]{1,0:T(8,128)S(1)}, f32[256,256]{1,0:T(8,128)}, u32[]{:S(2)}) copy-start(f32[256,256]{1,0:T(8,128)} %param.3) | copy-start | bytes 786436
  1.4 21.3 %collective-permute-start.6 = (f32[2,256]{1,0:T(2,128)S(1)}, f32[2,256]{1,0:T(2,128)S(1)}, u32[]{:S(2)}, u32[]{:S(2)}) collective-permute-start(f32[2,256]{1,0:T(2,128)S(1)} %add_convert_fusion), channel_id=1, source_target_pairs={{0,8},{1,9},{2,10},{3,11},{4,12},{5,13},{6,14},{7,15},{8,0},{9,1},... | collective-permute-start | bytes 6152 | tf_op jit(solution)/shard_map/ppermute | solution.py:13
  3.3 21.9 %collective-permute-start.4 = (f32[2,256]{1,0:T(2,128)S(1)}, f32[2,256]{1,0:T(2,128)S(1)}, u32[]{:S(2)}, u32[]{:S(2)}) collective-permute-start(f32[2,256]{1,0:T(2,128)S(1)} %add_convert_fusion), channel_id=1, source_target_pairs={{0,4},{1,5},{2,6},{3,7},{4,0},{5,1},{6,2},{7,3},{8,12},{9,13},{10,... | collective-permute-start | bytes 6152 | tf_op jit(solution)/shard_map/ppermute | solution.py:13
  8.4 18.7 %collective-permute-start.2 = (f32[2,256]{1,0:T(2,128)S(1)}, f32[2,256]{1,0:T(2,128)S(1)}, u32[]{:S(2)}, u32[]{:S(2)}) collective-permute-start(f32[2,256]{1,0:T(2,128)S(1)} %add_convert_fusion), channel_id=1, source_target_pairs={{0,2},{1,3},{2,0},{3,1},{4,6},{5,7},{6,4},{7,5},{8,10},{9,11},{10,... | collective-permute-start | bytes 6152 | tf_op jit(solution)/shard_map/ppermute | solution.py:13
  11.0 21.0 %collective-permute-start = (f32[2,256]{1,0:T(2,128)S(1)}, f32[2,256]{1,0:T(2,128)S(1)}, u32[]{:S(2)}, u32[]{:S(2)}) collective-permute-start(f32[2,256]{1,0:T(2,128)S(1)} %add_convert_fusion), channel_id=1, source_target_pairs={{0,1},{1,0},{2,3},{3,2},{4,5},{5,4},{6,7},{7,6},{8,9},{9,8},{10,11... | collective-permute-start | bytes 6152 | tf_op jit(solution)/shard_map/ppermute | solution.py:13
  14.3 21.0 %collective-permute-start.8 = (f32[2,256]{1,0:T(2,128)S(1)}, f32[2,256]{1,0:T(2,128)S(1)}, u32[]{:S(2)}, u32[]{:S(2)}) collective-permute-start(f32[2,256]{1,0:T(2,128)S(1)} %add_convert_fusion), channel_id=1, source_target_pairs={{0,16},{1,17},{2,18},{3,19},{4,20},{5,21},{6,22},{7,23},{8,24},{9,... | collective-permute-start | bytes 6152 | tf_op jit(solution)/shard_map/ppermute | solution.py:13
  18.8 1.0 copy-start.1
  22.7 15.7 %collective-permute-start.9 = (f32[2,256,256]{1,2,0:T(8,128)S(1)}, f32[2,256,256]{1,2,0:T(8,128)S(1)}, u32[]{:S(2)}, u32[]{:S(2)}) collective-permute-start(f32[2,256,256]{1,2,0:T(8,128)S(1)} %pad_maximum_fusion), channel_id=1, source_target_pairs={{0,16},{1,17},{2,18},{3,19},{4,20},{5,21},{6,22},{7,23},{8,24},{9,... | collective-permute-start | bytes 1572872 | tf_op jit(solution)/shard_map/ppermute | solution.py:13
  25.2 14.4 %collective-permute-start.7 = (f32[2,256,256]{1,2,0:T(8,128)S(1)}, f32[2,256,256]{1,2,0:T(8,128)S(1)}, u32[]{:S(2)}, u32[]{:S(2)}) collective-permute-start(f32[2,256,256]{1,2,0:T(8,128)S(1)} %pad_maximum_fusion), channel_id=1, source_target_pairs={{0,8},{1,9},{2,10},{3,11},{4,12},{5,13},{6,14},{7,15},{8,0},{9,1},... | collective-permute-start | bytes 1572872 | tf_op jit(solution)/shard_map/ppermute | solution.py:13
  27.1 18.1 %collective-permute-start.5 = (f32[2,256,256]{1,2,0:T(8,128)S(1)}, f32[2,256,256]{1,2,0:T(8,128)S(1)}, u32[]{:S(2)}, u32[]{:S(2)}) collective-permute-start(f32[2,256,256]{1,2,0:T(8,128)S(1)} %pad_maximum_fusion), channel_id=1, source_target_pairs={{0,4},{1,5},{2,6},{3,7},{4,0},{5,1},{6,2},{7,3},{8,12},{9,13},{10,... | collective-permute-start | bytes 1572872 | tf_op jit(solution)/shard_map/ppermute | solution.py:13
  32.0 24.9 %collective-permute-start.3 = (f32[2,256,256]{1,2,0:T(8,128)S(1)}, f32[2,256,256]{1,2,0:T(8,128)S(1)}, u32[]{:S(2)}, u32[]{:S(2)}) collective-permute-start(f32[2,256,256]{1,2,0:T(8,128)S(1)} %pad_maximum_fusion), channel_id=1, source_target_pairs={{0,2},{1,3},{2,0},{3,1},{4,6},{5,7},{6,4},{7,5},{8,10},{9,11},{10,... | collective-permute-start | bytes 1572872 | tf_op jit(solution)/shard_map/ppermute | solution.py:13
  35.4 22.8 %collective-permute-start.1 = (f32[2,256,256]{1,2,0:T(8,128)S(1)}, f32[2,256,256]{1,2,0:T(8,128)S(1)}, u32[]{:S(2)}, u32[]{:S(2)}) collective-permute-start(f32[2,256,256]{1,2,0:T(8,128)S(1)} %pad_maximum_fusion), channel_id=1, source_target_pairs={{0,1},{1,0},{2,3},{3,2},{4,5},{5,4},{6,7},{7,6},{8,9},{9,8},{10,11... | collective-permute-start | bytes 1572872 | tf_op jit(solution)/shard_map/ppermute | solution.py:13
  73.0 16.9 %collective-permute-start.14 = (f32[2,256]{1,0:T(2,128)S(1)}, f32[2,256]{1,0:T(2,128)S(1)}, u32[]{:S(2)}, u32[]{:S(2)}) collective-permute-start(f32[2,256]{1,0:T(2,128)S(1)} %pad_maximum_fusion.1), channel_id=1, source_target_pairs={{0,16},{1,17},{2,18},{3,19},{4,20},{5,21},{6,22},{7,23},{8,24},{9,... | collective-permute-start | bytes 6152 | tf_op jit(solution)/shard_map/ppermute | solution.py:13
  76.9 13.0 %collective-permute-start.13 = (f32[2,256]{1,0:T(2,128)S(1)}, f32[2,256]{1,0:T(2,128)S(1)}, u32[]{:S(2)}, u32[]{:S(2)}) collective-permute-start(f32[2,256]{1,0:T(2,128)S(1)} %pad_maximum_fusion.1), channel_id=1, source_target_pairs={{0,8},{1,9},{2,10},{3,11},{4,12},{5,13},{6,14},{7,15},{8,0},{9,1},... | collective-permute-start | bytes 6152 | tf_op jit(solution)/shard_map/ppermute | solution.py:13
  78.8 11.1 %collective-permute-start.12 = (f32[2,256]{1,0:T(2,128)S(1)}, f32[2,256]{1,0:T(2,128)S(1)}, u32[]{:S(2)}, u32[]{:S(2)}) collective-permute-start(f32[2,256]{1,0:T(2,128)S(1)} %pad_maximum_fusion.1), channel_id=1, source_target_pairs={{0,4},{1,5},{2,6},{3,7},{4,0},{5,1},{6,2},{7,3},{8,12},{9,13},{10,... | collective-permute-start | bytes 6152 | tf_op jit(solution)/shard_map/ppermute | solution.py:13
  82.0 8.0 %collective-permute-start.11 = (f32[2,256]{1,0:T(2,128)S(1)}, f32[2,256]{1,0:T(2,128)S(1)}, u32[]{:S(2)}, u32[]{:S(2)}) collective-permute-start(f32[2,256]{1,0:T(2,128)S(1)} %pad_maximum_fusion.1), channel_id=1, source_target_pairs={{0,2},{1,3},{2,0},{3,1},{4,6},{5,7},{6,4},{7,5},{8,10},{9,11},{10,... | collective-permute-start | bytes 6152 | tf_op jit(solution)/shard_map/ppermute | solution.py:13
  83.9 7.0 %collective-permute-start.10 = (f32[2,256]{1,0:T(2,128)S(1)}, f32[2,256]{1,0:T(2,128)S(1)}, u32[]{:S(2)}, u32[]{:S(2)}) collective-permute-start(f32[2,256]{1,0:T(2,128)S(1)} %pad_maximum_fusion.1), channel_id=1, source_target_pairs={{0,1},{1,0},{2,3},{3,2},{4,5},{5,4},{6,7},{7,6},{8,9},{9,8},{10,11... | collective-permute-start | bytes 6152 | tf_op jit(solution)/shard_map/ppermute | solution.py:13
  96.8 1.5 %copy-start.8 = (f32[256,256]{0,1:T(8,128)S(1)}, f32[256,256]{0,1:T(8,128)}, u32[]{:S(2)}) copy-start(f32[256,256]{0,1:T(8,128)} %get-tuple-element.63) | copy-start | bytes 786436
  98.3 1.0 copy-start.10
  99.2 0.9 copy-start.6
  100.2 0.9 copy-start.9
  101.1 0.9 copy-start.4
  102.1 0.9 copy-start.7
  103.0 0.9 copy-start.3
  104.0 0.9 copy-start.5
  104.9 0.9 copy-start.2
  104.9 1.0 copy-start.11
where the time goes:
time: 109 us; the launch traced here: 107 us
  starting transfers between devices  45.8 us (42%)
  matrix products  35.7 us (33%)
  waiting for transfers between devices  15.9 us (15%)
  local copies, waits for them, and re-layouts  6.57 us (6%)
  other arithmetic  2.18 us (2%)
  between operations  1.27 us (1%)
    ppermute x15, starting transfers between devices, from_partner(): lax.ppermute(x, axis, [(i, i ^ 1 << distance) for i in range(lax.axis_siz...  45.8 us
    dot_general x24, matrix products, scored(): jnp.dot(a, b.T, precision=lax.Precision.HIGHEST, preferred_element_type=j...  22.2 us
    ppermute x15, waiting for transfers between devices, from_partner(): lax.ppermute(x, axis, [(i, i ^ 1 << distance) for i in range(lax.axis_siz...  15.9 us
    dot_general x24, matrix products, applied(): jnp.dot(a, b, precision=lax.Precision.HIGHEST, preferred_element_type=jnp...  13.5 us
    unnamed x28, local copies, waits for them, and re-layouts  6.52 us
  transfers between devices with their start and end apart: 15, of which 4 were waited for; matrix products, arithmetic and copies ran while one was open for 11% of the time, Pallas kernels for 0%

commit v1 on v0

v1 whole, which is shorter than its diff:
```python
import math

import jax
import jax.numpy as jnp
from jax import lax
from jax.experimental import pallas as pl
from jax.experimental.pallas import tpu as pltpu
from jax.sharding import PartitionSpec as P

MESH = pl.DeviceIdType.MESH
F32, BF16 = jnp.float32, jnp.bfloat16

R = 256
D = 256
CHUNKS = 8
CR = 2 * R // CHUNKS
TAU = 0.5
LOGIT = 1.0 / (TAU * math.log(2.0))
WINDOW = 2
STEPS = 12


def flip(n, bit):
    return n + bit - 2 * bit * ((n // bit) % 2)


def split(x):
    hi = x.astype(BF16)
    return hi, (x - hi.astype(F32)).astype(BF16)


def dot_t(a, b):
    return lax.dot_general(a, b, (((1,), (1,)), ((), ())), preferred_element_type=F32)


def dot(a, b):
    return lax.dot_general(a, b, (((1,), (0,)), ((), ())), preferred_element_type=F32)


def kernel(
    one_hbm, two_hbm, ids_hbm, z, grad, inv_r,
    raw, zl_hi, zl_lo, core_z, streams, k_hi, k_lo, e_hi, e_lo, acc, den_acc, id_col, ids_int, ids, r_ids, id_rows,
    inv_row, r_inv, inv_rows, diag,
    load_sem, direct_send, direct_recv, fwd_send, fwd_recv, core_send, core_recv, ids_send, ids_recv, den_send, den_recv,
):
    blk, grp = lax.axis_index("blk"), lax.axis_index("grp")
    x1 = (flip(blk, 2), grp)
    x3 = (flip(blk, 2), flip(grp, 1))
    y1 = (blk, flip(grp, 2))
    y3 = (blk, flip(flip(grp, 2), 4))
    core = (flip(blk, 1), grp)
    x2 = (blk, flip(grp, 1))
    y2 = (blk, flip(grp, 4))
    partners = (x1, y1, x2, y2, core)

    barrier = pltpu.get_barrier_semaphore()
    for peer in (x1, x3, y1, y3, core, x2, y2):
        pl.semaphore_signal(barrier, inc=1, device_id=peer, device_id_type=MESH)

    loads = [
        pltpu.make_async_copy(one_hbm, raw.at[pl.ds(0, R)], load_sem.at[0]),
        pltpu.make_async_copy(two_hbm, raw.at[pl.ds(R, R)], load_sem.at[1]),
        pltpu.make_async_copy(ids_hbm, ids_int, load_sem.at[2]),
    ]
    for copy in loads:
        copy.start()

    def direct(axis, c):
        return pltpu.make_async_remote_copy(
            src_ref=z.at[pl.ds(CR * c, CR)],
            dst_ref=streams.at[c, axis],
            send_sem=direct_send.at[axis, c],
            recv_sem=direct_recv.at[axis, c],
            device_id=(x1, y1)[axis],
            device_id_type=MESH,
        )

    def forward(axis, c):
        return pltpu.make_async_remote_copy(
            src_ref=streams.at[c, axis],
            dst_ref=streams.at[c, 2 + axis],
            send_sem=fwd_send.at[axis, c],
            recv_sem=fwd_recv.at[axis, c],
            device_id=(x3, y3)[axis],
            device_id_type=MESH,
        )

    to_core = pltpu.make_async_remote_copy(
        src_ref=z, dst_ref=core_z, send_sem=core_send, recv_sem=core_recv, device_id=core, device_id_type=MESH
    )

    def send_ids(p):
        return pltpu.make_async_remote_copy(
            src_ref=ids, dst_ref=r_ids.at[p], send_sem=ids_send.at[p], recv_sem=ids_recv.at[p],
            device_id=partners[p], device_id_type=MESH,
        )

    def send_inv(p):
        return pltpu.make_async_remote_copy(
            src_ref=inv_row, dst_ref=r_inv.at[p], send_sem=den_send.at[p], recv_sem=den_recv.at[p],
            device_id=partners[p], device_id_type=MESH,
        )

    def normalise(c):
        rows = pl.ds(CR * c, CR)
        x = raw[rows]
        ir = lax.rsqrt(jnp.sum(x * x, axis=1, keepdims=True) + 1e-06)
        inv_r[rows] = ir
        z[rows] = x * ir

    loads[0].wait()
    for c in range(CHUNKS):
        if c == CHUNKS // 2:
            loads[1].wait()
        normalise(c)
        if c == 0:
            pl.semaphore_wait(barrier, 7)
        if c < WINDOW:
            direct(0, c).start()
            direct(1, c).start()
    loads[2].wait()
    for q in range(4):
        ids[pl.ds(2 * q, 2)] = ids_int[...].astype(F32)
    for p in range(5):
        send_ids(p).start()
    to_core.start()

    hi, lo = split(z[...] * LOGIT)
    zl_hi[...] = hi
    zl_lo[...] = lo
    d = jnp.exp2(LOGIT * jnp.sum(z[pl.ds(0, R)] * z[pl.ds(R, R)], axis=1, keepdims=True))
    diag[...] = d
    lane = lax.broadcasted_iota(jnp.int32, (R, 128), 1)
    start = jnp.where(lane == 0, d, 0.0)
    den_acc[pl.ds(0, R)] = start
    den_acc[pl.ds(R, R)] = start
    acc[...] = jnp.zeros_like(acc)
    for q in range(2):
        id_col[pl.ds(128 * q, 128)] = jnp.broadcast_to(ids[pl.ds(q, 1)], (128, 128)).T

    def scores(slot, keys, key_ids):
        hi, lo = split(keys)
        k_hi[slot] = hi
        k_lo[...] = lo
        keep = jnp.concatenate([id_col[...], id_col[...]], axis=1) != key_ids
        for h in range(2):
            rows = pl.ds(R * h, R)
            s = dot_t(zl_hi[rows], hi) + dot_t(zl_hi[rows], lo) + dot_t(zl_lo[rows], hi)
            e = jnp.where(keep, jnp.exp2(s), 0.0)
            den_acc[rows] += e[:, :128] + e[:, 128:]
            ehi, elo = split(e)
            e_hi[slot, rows] = ehi
            e_lo[rows] = elo

    def gather(slot):
        for h in range(2):
            rows = pl.ds(R * h, R)
            ehi = e_hi[slot, rows]
            acc[rows] += dot(ehi, k_hi[slot]) + dot(ehi, k_lo[...]) + dot(e_lo[rows], k_hi[slot])

    def pair_ids(ref):
        return jnp.concatenate([ref[pl.ds(0, 1)], ref[pl.ds(1, 1)]], axis=1)

    own_ids = pair_ids(ids)
    for h in range(2):
        scores(h, z[pl.ds(R * h, R)], own_ids)
        gather(h)

    def pass_on(c):
        for axis in range(2):
            direct(axis, c).wait_recv()
            forward(axis, c).start()

        def refill():
            for axis in range(2):
                direct(axis, c).wait_send()
                direct(axis, c + WINDOW).start()

        if isinstance(c, int):
            refill()
        else:
            pl.when(c + WINDOW < CHUNKS)(refill)

    for p in range(5):
        send_ids(p).wait_recv()
    to_core.wait_recv()
    pass_on(0)
    core_ids = pair_ids(r_ids.at[4])
    for h in range(2):
        scores(2 + h, core_z[pl.ds(R * h, R)], core_ids)
        gather(2 + h)
        if h == 0:
            pass_on(1)

    left = lax.broadcasted_iota(jnp.int32, (8, 128), 1) < 64

    def mixed(refs):
        a, b, c, d = (refs[p] for p in range(4))
        turn = lambda x: pltpu.roll(x, 64, 1)
        first = jnp.concatenate([jnp.where(left, a, turn(b)), jnp.where(left, c, turn(d))], axis=1)
        second = jnp.concatenate([jnp.where(left, turn(a), b), jnp.where(left, turn(c), d)], axis=1)
        return first, second

    first, second = mixed(r_ids)
    for q in range(2):
        id_rows[pl.ds(2 * q, 1)] = first[q : q + 1]
        id_rows[pl.ds(2 * q + 1, 1)] = second[q : q + 1]

    def arrived(c):
        for axis in range(2):
            forward(axis, c).wait_recv()

    def stream_scores(c):
        scores(4 + c, streams[c].reshape(4 * CR, D), id_rows[pl.ds(c % 4, 1)])

    def stream_step(c, carry):
        pass_on(c + 2)
        arrived(c)
        stream_scores(c)
        gather(4 + c)
        return carry

    lax.fori_loop(0, CHUNKS - 2, stream_step, 0)
    arrived(CHUNKS - 2)
    stream_scores(CHUNKS - 2)
    gather(4 + CHUNKS - 2)
    arrived(CHUNKS - 1)
    stream_scores(CHUNKS - 1)

    s_hi = den_acc[...].astype(BF16)
    rest = den_acc[...] - s_hi.astype(F32)
    s_mid, s_lo = split(rest)
    ones = jnp.ones((8, 128), BF16)
    sums = dot_t(ones, s_hi) + dot_t(ones, s_mid) + dot_t(ones, s_lo)
    own_inv = 1.0 / sums
    for q in range(4):
        inv_row[pl.ds(q, 1)] = own_inv[0:1, 128 * q : 128 * (q + 1)]
    for q in range(4):
        inv_row[pl.ds(4 + q, 1)] = own_inv[0:1, 128 * q : 128 * (q + 1)]
    for p in range(5):
        send_inv(p).start()

    gather(4 + CHUNKS - 1)
    centre = jnp.mean(own_inv[0:1], axis=1, keepdims=True)
    inv_col = 1.0 / jnp.sum(den_acc[...], axis=1, keepdims=True)
    coef = diag[...] * (inv_col[:R] + inv_col[R:]) - 1.0 / TAU
    for h in range(2):
        rows, others = pl.ds(R * h, R), pl.ds(R * (1 - h), R)
        acc[rows] = (inv_col[R * h : R * (h + 1)] + centre) * acc[rows] + coef * z[others]

    for p in range(5):
        send_inv(p).wait_recv()
    first, second = mixed(r_inv)
    for h in range(2):
        for q in range(2):
            lanes = pl.ds(128 * q, 128)
            inv_rows[pl.ds(h, 1), lanes] = inv_row[pl.ds(2 * h + q, 1)]
            inv_rows[pl.ds(2 + h, 1), lanes] = r_inv[4, pl.ds(2 * h + q, 1)]
    for q in range(4):
        inv_rows[pl.ds(4 + 2 * q, 1)] = first[q : q + 1]
        inv_rows[pl.ds(5 + 2 * q, 1)] = second[q : q + 1]

    for h in range(2):
        rows = pl.ds(R * h, R)
        g = acc[rows]
        for slot in range(STEPS):
            weight = (inv_rows[pl.ds(slot, 1)] - centre).astype(BF16)
            g = g + dot(e_hi[slot, rows] * weight, k_hi[slot])
        grad[rows] = g

    for c in range(CHUNKS):
        for axis in range(2):
            if c >= CHUNKS - WINDOW:
                direct(axis, c).wait_send()
            forward(axis, c).wait_send()
    to_core.wait_send()
    for p in range(5):
        send_ids(p).wait_send()
        send_inv(p).wait_send()


def finish(z, grad, inv_r, out_one, out_two, result, out_sem):
    outs = []
    for c in range(4):
        rows = pl.ds(128 * c, 128)
        g, own = grad[rows], z[rows]
        result[rows] = (g - own * jnp.sum(own * g, axis=1, keepdims=True)) * inv_r[rows]
        copy = pltpu.make_async_copy(
            result.at[rows], (out_one, out_two)[c // 2].at[pl.ds(128 * (c % 2), 128)], out_sem.at[c]
        )
        copy.start()
        outs.append(copy)
    for copy in outs:
        copy.wait()


def on_device(view_one, view_two, node_ids):
    dma = pltpu.SemaphoreType.DMA
    hbm = pl.BlockSpec(memory_space=pltpu.HBM)
    vmem = pl.BlockSpec(memory_space=pltpu.VMEM)
    middle = pl.pallas_call(
        kernel,
        out_shape=(
            pltpu.VMEM((2 * R, D), F32),
            pltpu.VMEM((2 * R, D), F32),
            pltpu.VMEM((2 * R, 1), F32),
        ),
        in_specs=[hbm] * 3,
        out_specs=(vmem,) * 3,
        scratch_shapes=[
            pltpu.VMEM((2 * R, D), F32),
            pltpu.VMEM((2 * R, D), BF16),
            pltpu.VMEM((2 * R, D), BF16),
            pltpu.VMEM((2 * R, D), F32),
            pltpu.VMEM((CHUNKS, 4, CR, D), F32),
            pltpu.VMEM((STEPS, 256, D), BF16),
            pltpu.VMEM((256, D), BF16),
            pltpu.VMEM((STEPS, 2 * R, 256), BF16),
            pltpu.VMEM((2 * R, 256), BF16),
            pltpu.VMEM((2 * R, D), F32),
            pltpu.VMEM((2 * R, 128), F32),
            pltpu.VMEM((R, 128), F32),
            pltpu.VMEM((2, 128), jnp.int32),
            pltpu.VMEM((8, 128), F32),
            pltpu.VMEM((5, 8, 128), F32),
            pltpu.VMEM((8, 256), F32),
            pltpu.VMEM((8, 128), F32),
            pltpu.VMEM((5, 8, 128), F32),
            pltpu.VMEM((16, 256), F32),
            pltpu.VMEM((R, 1), F32),
            dma((3,)),
            dma((2, CHUNKS)),
            dma((2, CHUNKS)),
            dma((2, CHUNKS)),
            dma((2, CHUNKS)),
            dma,
            dma,
            dma((5,)),
            dma((5,)),
            dma((5,)),
            dma((5,)),
        ],
        compiler_params=pltpu.CompilerParams(
            collective_id=0, has_side_effects=True, vmem_limit_bytes=48 * 1024 * 1024
        ),
    )(*(pltpu.with_memory_space_constraint(x, pltpu.HBM) for x in (view_one, view_two, node_ids.reshape(2, 128))))
    return pl.pallas_call(
        finish,
        out_shape=(jax.ShapeDtypeStruct((R, D), F32), jax.ShapeDtypeStruct((R, D), F32)),
        in_specs=[vmem] * 3,
        out_specs=(hbm, hbm),
        scratch_shapes=[pltpu.VMEM((2 * R, D), F32), dma((4,))],
    )(*middle)


def solution(mesh):
    rows = P(("blk", "grp"), None)
    return jax.shard_map(
        on_device,
        mesh=mesh,
        in_specs=(rows, rows, P(("blk", "grp"))),
        out_specs=(rows, rows),
        check_vma=False,
    )
```

time: 109 us -> 39.4 us (0.36)
  the two profiles are of different devices: /device:TPU:6 before, /device:TPU:2 now
where the time goes in v1:
time: 39.4 us; the launch traced here: 39.2 us
  Pallas kernels  36.3 us (92%)
  local copies, waits for them, and re-layouts  2.26 us (6%)
  between operations  0.65 us (2%)
    pallas_call x1, Pallas kernels, on_device(): pl.pallas_call(kernel, out_shape=(pltpu.VMEM((2 * R, D), F32), pltpu.VMEM...  34 us
    pallas_call x1, Pallas kernels, on_device(): pl.pallas_call(finish, out_shape=(jax.ShapeDtypeStruct((R, D), F32), jax....  2.27 us
    unnamed x6, local copies, waits for them, and re-layouts  2.26 us

profile of v1, /device:TPU:2, one launch (start us, length us, event | category | flops | bytes accessed | tf_op | source)
XLA Modules:
  0.0 39.2 jit_solution(14730876489047098165)
XLA Ops:
  0.6 34.0 %shard_map.50 = (f32[512,256]{1,0:T(8,128)S(1)}, f32[512,256]{1,0:T(8,128)S(1)}, f32[512,1]{1,0:T(8,128)S(1)}) custom-call(f32[256,256]{1,0:T(8,128)} %one_hbm.1, f32[256,256]{1,0:T(8,128)} %two_hbm.1, s32[2,128]{1,0:T(2,128)} %bitcast.1), custom_call_target="tpu_custom_call" | custom-call | tf_op jit(solution)/shard_map/pallas_call | solution.py:301
  34.7 0.0 copy-start
  34.7 0.8 %copy-done = f32[512,256]{1,0:T(8,128)} copy-done((f32[512,256]{1,0:T(8,128)}, f32[512,256]{1,0:T(8,128)S(1)}, u32[]{:S(2)}) %copy-start) | copy-done | bytes 524312
  35.5 0.0 copy-start.1
  35.5 0.8 %copy-done.1 = f32[512,256]{1,0:T(8,128)} copy-done((f32[512,256]{1,0:T(8,128)}, f32[512,256]{1,0:T(8,128)S(1)}, u32[]{:S(2)}) %copy-start.1) | copy-done | bytes 524312
  36.3 0.0 copy-start.2
  36.3 0.7 %copy-done.2 = f32[512,1]{1,0:T(8,128)} copy-done((f32[512,1]{1,0:T(8,128)}, f32[512,1]{1,0:T(8,128)S(1)}, u32[]{:S(2)}) %copy-start.2) | copy-done | bytes 2072
  37.0 2.3 %shard_map.51 = (f32[256,256]{1,0:T(8,128)}, f32[256,256]{1,0:T(8,128)}) custom-call(f32[512,256]{1,0:T(8,128)} %copy-done, f32[512,256]{1,0:T(8,128)} %copy-done.1, f32[512,1]{1,0:T(8,128)} %copy-done.2), custom_call_target="tpu_custom_call" | custom-call | tf_op jit(solution)/shard_map/pallas_call | solution.py:347
Async XLA Ops:
  34.7 0.8 %copy-start = (f32[512,256]{1,0:T(8,128)}, f32[512,256]{1,0:T(8,128)S(1)}, u32[]{:S(2)}) copy-start(f32[512,256]{1,0:T(8,128)S(1)} %get-tuple-element.5.z) | copy-start | bytes 1572868
  35.5 0.8 %copy-start.1 = (f32[512,256]{1,0:T(8,128)}, f32[512,256]{1,0:T(8,128)S(1)}, u32[]{:S(2)}) copy-start(f32[512,256]{1,0:T(8,128)S(1)} %get-tuple-element.6.grad) | copy-start | bytes 1572868
  36.3 0.7 %copy-start.2 = (f32[512,1]{1,0:T(8,128)}, f32[512,1]{1,0:T(8,128)S(1)}, u32[]{:S(2)}) copy-start(f32[512,1]{1,0:T(8,128)S(1)} %get-tuple-element.7.inv_r) | copy-start | bytes 6148

commit v2 on v1

--- a/solution.py
+++ b/solution.py
@@ -12,11 +12,12 @@
 
 R = 256
 D = 256
-CHUNKS = 8
+CHUNKS = 16
 CR = 2 * R // CHUNKS
+PAIRS = CHUNKS // 2
 TAU = 0.5
 LOGIT = 1.0 / (TAU * math.log(2.0))
-WINDOW = 2
+WINDOW = 6
 STEPS = 12
 
 
@@ -65,10 +66,13 @@
     for copy in loads:
         copy.start()
 
+    def piece(c, stream):
+        return streams.at[c // 2, stream, pl.ds(CR * (c % 2), CR)]
+
     def direct(axis, c):
         return pltpu.make_async_remote_copy(
             src_ref=z.at[pl.ds(CR * c, CR)],
-            dst_ref=streams.at[c, axis],
+            dst_ref=piece(c, axis),
             send_sem=direct_send.at[axis, c],
             recv_sem=direct_recv.at[axis, c],
             device_id=(x1, y1)[axis],
@@ -77,8 +81,8 @@
 
     def forward(axis, c):
         return pltpu.make_async_remote_copy(
-            src_ref=streams.at[c, axis],
-            dst_ref=streams.at[c, 2 + axis],
+            src_ref=piece(c, axis),
+            dst_ref=piece(c, 2 + axis),
             send_sem=fwd_send.at[axis, c],
             recv_sem=fwd_recv.at[axis, c],
             device_id=(x3, y3)[axis],
@@ -101,29 +105,31 @@
             device_id=partners[p], device_id_type=MESH,
         )
 
-    def normalise(c):
-        rows = pl.ds(CR * c, CR)
+    def normalise(first, count):
+        rows = pl.ds(first, count)
         x = raw[rows]
         ir = lax.rsqrt(jnp.sum(x * x, axis=1, keepdims=True) + 1e-06)
         inv_r[rows] = ir
         z[rows] = x * ir
 
+    def launch(c):
+        direct(0, c).start()
+        direct(1, c).start()
+
     loads[0].wait()
-    for c in range(CHUNKS):
-        if c == CHUNKS // 2:
-            loads[1].wait()
-        normalise(c)
-        if c == 0:
-            pl.semaphore_wait(barrier, 7)
-        if c < WINDOW:
-            direct(0, c).start()
-            direct(1, c).start()
+    normalise(0, 2 * CR)
+    pl.semaphore_wait(barrier, 7)
+    launch(0)
+    normalise(2 * CR, R - 2 * CR)
+    launch(1)
+    loads[1].wait()
     loads[2].wait()
     for q in range(4):
         ids[pl.ds(2 * q, 2)] = ids_int[...].astype(F32)
     for p in range(5):
         send_ids(p).start()
-    to_core.start()
+    normalise(R, R)
+    launch(2)
 
     hi, lo = split(z[...] * LOGIT)
     zl_hi[...] = hi
@@ -134,37 +140,29 @@
     start = jnp.where(lane == 0, d, 0.0)
     den_acc[pl.ds(0, R)] = start
     den_acc[pl.ds(R, R)] = start
-    acc[...] = jnp.zeros_like(acc)
     for q in range(2):
         id_col[pl.ds(128 * q, 128)] = jnp.broadcast_to(ids[pl.ds(q, 1)], (128, 128)).T
 
     def scores(slot, keys, key_ids):
-        hi, lo = split(keys)
-        k_hi[slot] = hi
-        k_lo[...] = lo
+        place = pl.ds(pl.multiple_of(256 * slot, 256), 256)
+        khi, klo = split(keys)
+        k_hi[place] = khi
+        k_lo[place] = klo
         keep = jnp.concatenate([id_col[...], id_col[...]], axis=1) != key_ids
-        for h in range(2):
-            rows = pl.ds(R * h, R)
-            s = dot_t(zl_hi[rows], hi) + dot_t(zl_hi[rows], lo) + dot_t(zl_lo[rows], hi)
-            e = jnp.where(keep, jnp.exp2(s), 0.0)
-            den_acc[rows] += e[:, :128] + e[:, 128:]
-            ehi, elo = split(e)
-            e_hi[slot, rows] = ehi
-            e_lo[rows] = elo
-
-    def gather(slot):
-        for h in range(2):
-            rows = pl.ds(R * h, R)
-            ehi = e_hi[slot, rows]
-            acc[rows] += dot(ehi, k_hi[slot]) + dot(ehi, k_lo[...]) + dot(e_lo[rows], k_hi[slot])
+        s = dot_t(zl_hi[...], khi) + dot_t(zl_hi[...], klo) + dot_t(zl_lo[...], khi)
+        e = jnp.where(jnp.concatenate([keep, keep], axis=0), jnp.exp2(s), 0.0)
+        den_acc[...] += e[:, :128] + e[:, 128:]
+        ehi, elo = split(e)
+        e_hi[:, place] = ehi
+        e_lo[:, place] = elo
+
+    def gather(first, count):
+        place = pl.ds(256 * first, 256 * count)
+        part = dot(e_hi[:, place], k_hi[place]) + dot(e_hi[:, place], k_lo[place]) + dot(e_lo[:, place], k_hi[place])
+        acc[...] = part if first == 0 else acc[...] + part
 
     def pair_ids(ref):
         return jnp.concatenate([ref[pl.ds(0, 1)], ref[pl.ds(1, 1)]], axis=1)
-
-    own_ids = pair_ids(ids)
-    for h in range(2):
-        scores(h, z[pl.ds(R * h, R)], own_ids)
-        gather(h)
 
     def pass_on(c):
         for axis in range(2):
@@ -181,16 +179,23 @@
         else:
             pl.when(c + WINDOW < CHUNKS)(refill)
 
+    launch(3)
+    own_ids = pair_ids(ids)
+    scores(0, z[pl.ds(0, R)], own_ids)
+    launch(4)
+    to_core.start()
+    scores(1, z[pl.ds(R, R)], own_ids)
+    launch(5)
+    pass_on(0)
+    pass_on(1)
     for p in range(5):
         send_ids(p).wait_recv()
     to_core.wait_recv()
-    pass_on(0)
     core_ids = pair_ids(r_ids.at[4])
-    for h in range(2):
-        scores(2 + h, core_z[pl.ds(R * h, R)], core_ids)
-        gather(2 + h)
-        if h == 0:
-            pass_on(1)
+    scores(2, core_z[pl.ds(0, R)], core_ids)
+    pass_on(2)
+    pass_on(3)
+    scores(3, core_z[pl.ds(R, R)], core_ids)
 
     left = lax.broadcasted_iota(jnp.int32, (8, 128), 1) < 64
 
@@ -206,26 +211,26 @@
         id_rows[pl.ds(2 * q, 1)] = first[q : q + 1]
         id_rows[pl.ds(2 * q + 1, 1)] = second[q : q + 1]
 
-    def arrived(c):
+    def stream_scores(p):
         for axis in range(2):
-            forward(axis, c).wait_recv()
-
-    def stream_scores(c):
-        scores(4 + c, streams[c].reshape(4 * CR, D), id_rows[pl.ds(c % 4, 1)])
-
-    def stream_step(c, carry):
-        pass_on(c + 2)
-        arrived(c)
-        stream_scores(c)
-        gather(4 + c)
+            forward(axis, 2 * p).wait_recv()
+            forward(axis, 2 * p + 1).wait_recv()
+        scores(4 + p, streams[p].reshape(8 * CR, D), id_rows[pl.ds(p % 4, 1)])
+
+    def stream_step(p, carry):
+        pass_on(2 * p)
+        pass_on(2 * p + 1)
+        stream_scores(p - 2)
         return carry
 
-    lax.fori_loop(0, CHUNKS - 2, stream_step, 0)
-    arrived(CHUNKS - 2)
-    stream_scores(CHUNKS - 2)
-    gather(4 + CHUNKS - 2)
-    arrived(CHUNKS - 1)
-    stream_scores(CHUNKS - 1)
+    pass_on(4)
+    pass_on(5)
+    gather(0, 4)
+    stream_scores(0)
+    lax.fori_loop(3, PAIRS, stream_step, 0)
+    stream_scores(PAIRS - 2)
+    gather(4, 6)
+    stream_scores(PAIRS - 1)
 
     s_hi = den_acc[...].astype(BF16)
     rest = den_acc[...] - s_hi.astype(F32)
@@ -240,7 +245,7 @@
     for p in range(5):
         send_inv(p).start()
 
-    gather(4 + CHUNKS - 1)
+    gather(10, 2)
     centre = jnp.mean(own_inv[0:1], axis=1, keepdims=True)
     inv_col = 1.0 / jnp.sum(den_acc[...], axis=1, keepdims=True)
     coef = diag[...] * (inv_col[:R] + inv_col[R:]) - 1.0 / TAU
@@ -251,22 +256,21 @@
     for p in range(5):
         send_inv(p).wait_recv()
     first, second = mixed(r_inv)
-    for h in range(2):
-        for q in range(2):
-            lanes = pl.ds(128 * q, 128)
-            inv_rows[pl.ds(h, 1), lanes] = inv_row[pl.ds(2 * h + q, 1)]
-            inv_rows[pl.ds(2 + h, 1), lanes] = r_inv[4, pl.ds(2 * h + q, 1)]
+
+    def spread(slot, row, lane, values):
+        inv_rows[:, pl.ds(256 * slot + lane, values.shape[1])] = jnp.broadcast_to(values[row : row + 1] - centre, (16, values.shape[1])).astype(BF16)
+
+    own, other = inv_row[...], r_inv[4]
     for q in range(4):
-        inv_rows[pl.ds(4 + 2 * q, 1)] = first[q : q + 1]
-        inv_rows[pl.ds(5 + 2 * q, 1)] = second[q : q + 1]
+        spread(q // 2, q, 128 * (q % 2), own)
+        spread(2 + q // 2, q, 128 * (q % 2), other)
+        spread(4 + 2 * q, q, 0, first)
+        spread(5 + 2 * q, q, 0, second)
 
     for h in range(2):
         rows = pl.ds(R * h, R)
-        g = acc[rows]
-        for slot in range(STEPS):
-            weight = (inv_rows[pl.ds(slot, 1)] - centre).astype(BF16)
-            g = g + dot(e_hi[slot, rows] * weight, k_hi[slot])
-        grad[rows] = g
+        weight = jnp.broadcast_to(inv_rows[0:1], (R, 256 * STEPS))
+        grad[rows] = acc[rows] + dot(e_hi[rows] * weight, k_hi[...])
 
     for c in range(CHUNKS):
         for axis in range(2):
@@ -312,11 +316,11 @@
             pltpu.VMEM((2 * R, D), BF16),
             pltpu.VMEM((2 * R, D), BF16),
             pltpu.VMEM((2 * R, D), F32),
-            pltpu.VMEM((CHUNKS, 4, CR, D), F32),
-            pltpu.VMEM((STEPS, 256, D), BF16),
-            pltpu.VMEM((256, D), BF16),
-            pltpu.VMEM((STEPS, 2 * R, 256), BF16),
-            pltpu.VMEM((2 * R, 256), BF16),
+            pltpu.VMEM((PAIRS, 4, 2 * CR, D), F32),
+            pltpu.VMEM((256 * STEPS, D), BF16),
+            pltpu.VMEM((256 * STEPS, D), BF16),
+            pltpu.VMEM((2 * R, 256 * STEPS), BF16),
+            pltpu.VMEM((2 * R, 256 * STEPS), BF16),
             pltpu.VMEM((2 * R, D), F32),
             pltpu.VMEM((2 * R, 128), F32),
             pltpu.VMEM((R, 128), F32),
@@ -326,7 +330,7 @@
             pltpu.VMEM((8, 256), F32),
             pltpu.VMEM((8, 128), F32),
             pltpu.VMEM((5, 8, 128), F32),
-            pltpu.VMEM((16, 256), F32),
+            pltpu.VMEM((16, 256 * STEPS), BF16),
             pltpu.VMEM((R, 1), F32),
             dma((3,)),
             dma((2, CHUNKS)),
@@ -341,7 +345,7 @@
             dma((5,)),
         ],
         compiler_params=pltpu.CompilerParams(
-            collective_id=0, has_side_effects=True, vmem_limit_bytes=48 * 1024 * 1024
+            collective_id=0, has_side_effects=True, vmem_limit_bytes=32 * 1024 * 1024
         ),
     )(*(pltpu.with_memory_space_constraint(x, pltpu.HBM) for x in (view_one, view_two, node_ids.reshape(2, 128))))
     return pl.pallas_call(
@@ -350,6 +354,7 @@
         in_specs=[vmem] * 3,
         out_specs=(hbm, hbm),
         scratch_shapes=[pltpu.VMEM((2 * R, D), F32), dma((4,))],
+        compiler_params=pltpu.CompilerParams(vmem_limit_bytes=4 * 1024 * 1024),
     )(*middle)
 
 

time: 39.4 us -> 35.7 us (0.906)
  the two profiles are of different devices: /device:TPU:2 before, /device:TPU:6 now
where the time goes in v2:
time: 35.7 us; the launch traced here: 35.5 us
  Pallas kernels  34.9 us (98%)
  between operations  0.64 us (2%)
    pallas_call x1, Pallas kernels, on_device(): pl.pallas_call(kernel, out_shape=(pltpu.VMEM((2 * R, D), F32), pltpu.VMEM...  33.9 us
    pallas_call x1, Pallas kernels, on_device(): pl.pallas_call(finish, out_shape=(jax.ShapeDtypeStruct((R, D), F32), jax....  1 us

profile of v2, /device:TPU:6, one launch (start us, length us, event | category | flops | bytes accessed | tf_op | source)
XLA Modules:
  0.0 35.5 jit_solution(17019015573338253227)
XLA Ops:
  0.6 33.9 %shard_map.50 = (f32[512,256]{1,0:T(8,128)S(1)}, f32[512,256]{1,0:T(8,128)S(1)}, f32[512,1]{1,0:T(8,128)S(1)}) custom-call(f32[256,256]{1,0:T(8,128)} %one_hbm.1, f32[256,256]{1,0:T(8,128)} %two_hbm.1, s32[2,128]{1,0:T(2,128)} %bitcast.1), custom_call_target="tpu_custom_call" | custom-call | tf_op jit(solution)/shard_map/pallas_call | solution.py:305
  34.5 1.0 %shard_map.51 = (f32[256,256]{1,0:T(8,128)}, f32[256,256]{1,0:T(8,128)}) custom-call(f32[512,256]{1,0:T(8,128)S(1)} %get-tuple-element.5.z, f32[512,256]{1,0:T(8,128)S(1)} %get-tuple-element.6.grad, f32[512,1]{1,0:T(8,128)S(1)} %get-tuple-element.7.inv_r), custom_call_target="tpu_custom_call" | custom-call | tf_op jit(solution)/shard_map/pallas_call | solution.py:351

commit v3 on v2

v3 whole, which is shorter than its diff:
```python
import math

import jax
import jax.numpy as jnp
from jax import lax
from jax.experimental import pallas as pl
from jax.experimental.pallas import tpu as pltpu
from jax.sharding import PartitionSpec as P

MESH = pl.DeviceIdType.MESH
F32, BF16 = jnp.float32, jnp.bfloat16

R = 256
D = 256
CHUNKS = 8
CR = 2 * R // CHUNKS
TAU = 0.5
LOGIT = 1.0 / (TAU * math.log(2.0))
WINDOW = 3
STEPS = 12


def flip(n, bit):
    return n + bit - 2 * bit * ((n // bit) % 2)


def split(x):
    hi = x.astype(BF16)
    return hi, (x - hi.astype(F32)).astype(BF16)


def dot_t(a, b):
    return lax.dot_general(a, b, (((1,), (1,)), ((), ())), preferred_element_type=F32)


def dot(a, b):
    return lax.dot_general(a, b, (((1,), (0,)), ((), ())), preferred_element_type=F32)


def kernel(
    one_hbm, two_hbm, ids_hbm, z, grad, inv_r,
    raw, zl, core_z, streams, keys_all, e_all, acc, key_sum, den_acc, id_col, ids_int, ids, r_ids, id_rows,
    inv_row, r_inv, inv_rows, diag,
    load_sem, direct_send, direct_recv, fwd_send, fwd_recv, core_send, core_recv, ids_send, ids_recv, den_send, den_recv,
):
    blk, grp = lax.axis_index("blk"), lax.axis_index("grp")
    x1 = (flip(blk, 2), grp)
    x3 = (flip(blk, 2), flip(grp, 1))
    y1 = (blk, flip(grp, 2))
    y3 = (blk, flip(flip(grp, 2), 4))
    core = (flip(blk, 1), grp)
    x2 = (blk, flip(grp, 1))
    y2 = (blk, flip(grp, 4))
    partners = (x1, y1, x2, y2, core)

    barrier = pltpu.get_barrier_semaphore()
    for peer in (x1, x3, y1, y3, core, x2, y2):
        pl.semaphore_signal(barrier, inc=1, device_id=peer, device_id_type=MESH)

    loads = [
        pltpu.make_async_copy(one_hbm, raw.at[pl.ds(0, R)], load_sem.at[0]),
        pltpu.make_async_copy(two_hbm, raw.at[pl.ds(R, R)], load_sem.at[1]),
        pltpu.make_async_copy(ids_hbm, ids_int, load_sem.at[2]),
    ]
    for copy in loads:
        copy.start()

    def direct(axis, c):
        return pltpu.make_async_remote_copy(
            src_ref=z.at[pl.ds(CR * c, CR)],
            dst_ref=streams.at[c, axis],
            send_sem=direct_send.at[axis],
            recv_sem=direct_recv.at[axis, c],
            device_id=(x1, y1)[axis],
            device_id_type=MESH,
        )

    def forward(axis, c):
        return pltpu.make_async_remote_copy(
            src_ref=streams.at[c, axis],
            dst_ref=streams.at[c, 2 + axis],
            send_sem=fwd_send.at[axis],
            recv_sem=fwd_recv.at[axis, c],
            device_id=(x3, y3)[axis],
            device_id_type=MESH,
        )

    def to_core(h):
        rows = pl.ds(R * h, R)
        return pltpu.make_async_remote_copy(
            src_ref=z.at[rows], dst_ref=core_z.at[rows], send_sem=core_send, recv_sem=core_recv.at[h],
            device_id=core, device_id_type=MESH,
        )

    def whole(ref, send, recv):
        return pltpu.make_async_remote_copy(
            src_ref=ref, dst_ref=ref, send_sem=send, recv_sem=recv, device_id=core, device_id_type=MESH
        )

    def send_ids(p):
        return pltpu.make_async_remote_copy(
            src_ref=ids, dst_ref=r_ids.at[p], send_sem=ids_send, recv_sem=ids_recv,
            device_id=partners[p], device_id_type=MESH,
        )

    def send_inv(p):
        return pltpu.make_async_remote_copy(
            src_ref=inv_row, dst_ref=r_inv.at[p], send_sem=den_send, recv_sem=den_recv,
            device_id=partners[p], device_id_type=MESH,
        )

    def normalise(first, count):
        rows = pl.ds(first, count)
        x = raw[rows]
        ir = lax.rsqrt(jnp.sum(x * x, axis=1, keepdims=True) + 1e-06)
        inv_r[rows] = ir
        z[rows] = x * ir

    def launch(c):
        direct(0, c).start()
        direct(1, c).start()

    loads[0].wait()
    normalise(0, CR)
    pl.semaphore_wait(barrier, 7)
    launch(0)
    normalise(CR, R - CR)
    to_core(0).start()
    loads[1].wait()
    loads[2].wait()
    for q in range(4):
        ids[pl.ds(2 * q, 2)] = ids_int[...].astype(F32)
    for p in range(5):
        send_ids(p).start()
    normalise(R, R)
    launch(1)
    to_core(1).start()

    zl[...] = (z[...] * LOGIT).astype(BF16)
    d = jnp.exp2(LOGIT * jnp.sum(z[pl.ds(0, R)] * z[pl.ds(R, R)], axis=1, keepdims=True))
    diag[...] = d
    lane = lax.broadcasted_iota(jnp.int32, (R, 128), 1)
    start = jnp.where(lane == 0, d, 0.0)
    den_acc[pl.ds(0, R)] = start
    den_acc[pl.ds(R, R)] = start
    key_sum[...] = jnp.zeros_like(key_sum)
    for q in range(2):
        id_col[pl.ds(128 * q, 128)] = jnp.broadcast_to(ids[pl.ds(q, 1)], (128, 128)).T

    def scores(slot, keys, key_ids):
        place = pl.ds(pl.multiple_of(256 * slot, 256), 256)
        narrow = keys.astype(BF16)
        keys_all[place] = narrow
        key_sum[...] += jnp.sum(keys.reshape(32, 8, D), axis=0)
        keep = jnp.concatenate([id_col[...], id_col[...]], axis=1) != key_ids
        e = jnp.where(jnp.concatenate([keep, keep], axis=0), jnp.exp2(dot_t(zl[...], narrow)), 0.0)
        den_acc[...] += e[:, :128] + e[:, 128:]
        e_all[:, place] = (e - 1.0).astype(BF16)

    def gather(group):
        place = pl.ds(1024 * group, 1024)
        part = dot(e_all[:, place], keys_all[place])
        acc[...] = part if group == 0 else acc[...] + part

    def pair_ids(ref):
        return jnp.concatenate([ref[pl.ds(0, 1)], ref[pl.ds(1, 1)]], axis=1)

    def pass_on(c):
        for axis in range(2):
            direct(axis, c).wait_recv()
            forward(axis, c).start()
        if isinstance(c, int):
            launch(c + WINDOW)
        else:
            pl.when(c + WINDOW < CHUNKS)(lambda: launch(c + WINDOW))

    own_ids = pair_ids(ids)
    scores(0, z[pl.ds(0, R)], own_ids)
    launch(2)
    scores(1, z[pl.ds(R, R)], own_ids)
    pass_on(0)
    whole(r_ids, ids_send, ids_recv).wait_recv()
    core_ids = pair_ids(r_ids.at[4])
    to_core(0).wait_recv()
    scores(2, core_z[pl.ds(0, R)], core_ids)
    pass_on(1)
    to_core(1).wait_recv()
    scores(3, core_z[pl.ds(R, R)], core_ids)
    gather(0)

    left = lax.broadcasted_iota(jnp.int32, (8, 128), 1) < 64

    def mixed(refs):
        a, b, c, d = (refs[p] for p in range(4))
        turn = lambda x: pltpu.roll(x, 64, 1)
        first = jnp.concatenate([jnp.where(left, a, turn(b)), jnp.where(left, c, turn(d))], axis=1)
        second = jnp.concatenate([jnp.where(left, turn(a), b), jnp.where(left, turn(c), d)], axis=1)
        return first, second

    first, second = mixed(r_ids)
    for q in range(2):
        id_rows[pl.ds(2 * q, 1)] = first[q : q + 1]
        id_rows[pl.ds(2 * q + 1, 1)] = second[q : q + 1]

    def arrived(c):
        for axis in range(2):
            forward(axis, c).wait_recv()

    def stream_scores(c):
        scores(4 + c, streams[c].reshape(4 * CR, D), id_rows[pl.ds(c % 4, 1)])

    def stream_step(c, carry):
        pass_on(c + 2)
        arrived(c)
        stream_scores(c)
        return carry

    lax.fori_loop(0, 4, stream_step, 0)
    gather(1)
    lax.fori_loop(4, CHUNKS - 2, stream_step, 0)
    for c in range(CHUNKS - 2, CHUNKS):
        arrived(c)
        stream_scores(c)

    s_hi = den_acc[...].astype(BF16)
    rest = den_acc[...] - s_hi.astype(F32)
    s_mid, s_lo = split(rest)
    ones = jnp.ones((8, 128), BF16)
    sums = dot_t(ones, s_hi) + dot_t(ones, s_mid) + dot_t(ones, s_lo)
    own_inv = 1.0 / sums
    for q in range(4):
        inv_row[pl.ds(q, 1)] = own_inv[0:1, 128 * q : 128 * (q + 1)]
    for q in range(4):
        inv_row[pl.ds(4 + q, 1)] = own_inv[0:1, 128 * q : 128 * (q + 1)]
    for p in range(5):
        send_inv(p).start()

    gather(2)
    centre = jnp.mean(own_inv[0:1], axis=1, keepdims=True)
    inv_col = 1.0 / jnp.sum(den_acc[...], axis=1, keepdims=True)
    coef = diag[...] * (inv_col[:R] + inv_col[R:]) - 1.0 / TAU
    for h in range(2):
        rows, others = pl.ds(R * h, R), pl.ds(R * (1 - h), R)
        total = acc[rows] + jnp.sum(key_sum[...], axis=0, keepdims=True)
        acc[rows] = (inv_col[R * h : R * (h + 1)] + centre) * total + coef * z[others]

    def spread(slot, row, lane, values):
        inv_rows[0:1, pl.ds(256 * slot + lane, values.shape[1])] = values[row : row + 1] - centre

    def weighted(first, count):
        place = pl.ds(256 * first, 256 * count)
        off = jnp.broadcast_to(inv_rows[0:1, place], (16, 256 * count)).astype(BF16)[None]
        e = e_all[:, place].reshape(2 * R // 16, 16, 256 * count)
        return dot((e * off + off).reshape(2 * R, 256 * count), keys_all[place])

    own = inv_row[...]
    for q in range(4):
        spread(q // 2, q, 128 * (q % 2), own)
    acc[...] += weighted(0, 2)

    whole(r_inv, den_send, den_recv).wait_recv()
    first, second = mixed(r_inv)
    other = r_inv[4]
    for q in range(4):
        spread(2 + q // 2, q, 128 * (q % 2), other)
        spread(4 + 2 * q, q, 0, first)
        spread(5 + 2 * q, q, 0, second)
    grad[...] = acc[...] + weighted(2, STEPS - 2)

    for axis in range(2):
        whole(z, direct_send.at[axis], core_recv.at[0]).wait_send()
        whole(z, fwd_send.at[axis], core_recv.at[0]).wait_send()
    whole(z, core_send, core_recv.at[0]).wait_send()
    whole(r_ids, ids_send, ids_recv).wait_send()
    whole(r_inv, den_send, den_recv).wait_send()


def finish(z, grad, inv_r, out_one, out_two, result, out_sem):
    outs = []
    for c in range(4):
        rows = pl.ds(128 * c, 128)
        g, own = grad[rows], z[rows]
        result[rows] = (g - own * jnp.sum(own * g, axis=1, keepdims=True)) * inv_r[rows]
        copy = pltpu.make_async_copy(
            result.at[rows], (out_one, out_two)[c // 2].at[pl.ds(128 * (c % 2), 128)], out_sem.at[c]
        )
        copy.start()
        outs.append(copy)
    for copy in outs:
        copy.wait()


def on_device(view_one, view_two, node_ids):
    dma = pltpu.SemaphoreType.DMA
    hbm = pl.BlockSpec(memory_space=pltpu.HBM)
    vmem = pl.BlockSpec(memory_space=pltpu.VMEM)
    middle = pl.pallas_call(
        kernel,
        out_shape=(
            pltpu.VMEM((2 * R, D), F32),
            pltpu.VMEM((2 * R, D), F32),
            pltpu.VMEM((2 * R, 1), F32),
        ),
        in_specs=[hbm] * 3,
        out_specs=(vmem,) * 3,
        scratch_shapes=[
            pltpu.VMEM((2 * R, D), F32),
            pltpu.VMEM((2 * R, D), BF16),
            pltpu.VMEM((2 * R, D), F32),
            pltpu.VMEM((CHUNKS, 4, CR, D), F32),
            pltpu.VMEM((256 * STEPS, D), BF16),
            pltpu.VMEM((2 * R, 256 * STEPS), BF16),
            pltpu.VMEM((2 * R, D), F32),
            pltpu.VMEM((8, D), F32),
            pltpu.VMEM((2 * R, 128), F32),
            pltpu.VMEM((R, 128), F32),
            pltpu.VMEM((2, 128), jnp.int32),
            pltpu.VMEM((8, 128), F32),
            pltpu.VMEM((5, 8, 128), F32),
            pltpu.VMEM((8, 256), F32),
            pltpu.VMEM((8, 128), F32),
            pltpu.VMEM((5, 8, 128), F32),
            pltpu.VMEM((8, 256 * STEPS), F32),
            pltpu.VMEM((R, 1), F32),
            dma((3,)),
            dma((2,)),
            dma((2, CHUNKS)),
            dma((2,)),
            dma((2, CHUNKS)),
            dma,
            dma((2,)),
            dma,
            dma,
            dma,
            dma,
        ],
        compiler_params=pltpu.CompilerParams(
            collective_id=0, has_side_effects=True, vmem_limit_bytes=32 * 1024 * 1024
        ),
    )(*(pltpu.with_memory_space_constraint(x, pltpu.HBM) for x in (view_one, view_two, node_ids.reshape(2, 128))))
    return pl.pallas_call(
        finish,
        out_shape=(jax.ShapeDtypeStruct((R, D), F32), jax.ShapeDtypeStruct((R, D), F32)),
        in_specs=[vmem] * 3,
        out_specs=(hbm, hbm),
        scratch_shapes=[pltpu.VMEM((2 * R, D), F32), dma((4,))],
        compiler_params=pltpu.CompilerParams(vmem_limit_bytes=4 * 1024 * 1024),
    )(*middle)


def solution(mesh):
    rows = P(("blk", "grp"), None)
    return jax.shard_map(
        on_device,
        mesh=mesh,
        in_specs=(rows, rows, P(("blk", "grp"))),
        out_specs=(rows, rows),
        check_vma=False,
    )
```

time: 35.7 us -> 32.5 us (0.910)
  Pallas kernels: 34.9 us -> 31.6 us
    pallas_call x1, Pallas kernels: 33.9 us -> 30.6 us  [on_device(): pl.pallas_call(kernel, out_shape=(pltpu.VMEM((2 * R, D), F32), pltpu.VMEM...]
where the time goes in v3:
time: 32.5 us; the launch traced here: 32.2 us
  Pallas kernels  31.6 us (97%)
  between operations  0.64 us (2%)
    pallas_call x1, Pallas kernels, on_device(): pl.pallas_call(kernel, out_shape=(pltpu.VMEM((2 * R, D), F32), pltpu.VMEM...  30.6 us
    pallas_call x1, Pallas kernels, on_device(): pl.pallas_call(finish, out_shape=(jax.ShapeDtypeStruct((R, D), F32), jax....  1 us

profile of v3, /device:TPU:6, one launch (start us, length us, event | category | flops | bytes accessed | tf_op | source)
XLA Modules:
  0.0 32.2 jit_solution(1824918222703973972)
XLA Ops:
  0.6 30.6 %shard_map.50 = (f32[512,256]{1,0:T(8,128)S(1)}, f32[512,256]{1,0:T(8,128)S(1)}, f32[512,1]{1,0:T(8,128)S(1)}) custom-call(f32[256,256]{1,0:T(8,128)} %one_hbm.1, f32[256,256]{1,0:T(8,128)} %two_hbm.1, s32[2,128]{1,0:T(2,128)} %bitcast.1), custom_call_target="tpu_custom_call" | custom-call | tf_op jit(solution)/shard_map/pallas_call | solution.py:297
  31.2 1.0 %shard_map.51 = (f32[256,256]{1,0:T(8,128)}, f32[256,256]{1,0:T(8,128)}) custom-call(f32[512,256]{1,0:T(8,128)S(1)} %get-tuple-element.5.z, f32[512,256]{1,0:T(8,128)S(1)} %get-tuple-element.6.grad, f32[512,1]{1,0:T(8,128)S(1)} %get-tuple-element.7.inv_r), custom_call_target="tpu_custom_call" | custom-call | tf_op jit(solution)/shard_map/pallas_call | solution.py:341

commit v4 on v3

--- a/solution.py
+++ b/solution.py
@@ -16,7 +16,6 @@
 CR = 2 * R // CHUNKS
 TAU = 0.5
 LOGIT = 1.0 / (TAU * math.log(2.0))
-WINDOW = 3
 STEPS = 12
 
 
@@ -54,7 +53,7 @@
     partners = (x1, y1, x2, y2, core)
 
     barrier = pltpu.get_barrier_semaphore()
-    for peer in (x1, x3, y1, y3, core, x2, y2):
+    for peer in (x1, x3, y1, y3, core):
         pl.semaphore_signal(barrier, inc=1, device_id=peer, device_id_type=MESH)
 
     loads = [
@@ -65,26 +64,28 @@
     for copy in loads:
         copy.start()
 
-    def direct(axis, c):
-        return pltpu.make_async_remote_copy(
-            src_ref=z.at[pl.ds(CR * c, CR)],
-            dst_ref=streams.at[c, axis],
+    def direct(axis, c, first=0, count=CR, sem=None):
+        return pltpu.make_async_remote_copy(
+            src_ref=z.at[pl.ds(CR * c + first, count)],
+            dst_ref=streams.at[c, axis, pl.ds(first, count)],
             send_sem=direct_send.at[axis],
-            recv_sem=direct_recv.at[axis, c],
+            recv_sem=direct_recv.at[axis, c if sem is None else sem],
             device_id=(x1, y1)[axis],
             device_id_type=MESH,
         )
 
-    def forward(axis, c):
-        return pltpu.make_async_remote_copy(
-            src_ref=streams.at[c, axis],
-            dst_ref=streams.at[c, 2 + axis],
+    def forward(axis, c, first=0, count=CR, sem=None):
+        return pltpu.make_async_remote_copy(
+            src_ref=streams.at[c, axis, pl.ds(first, count)],
+            dst_ref=streams.at[c, 2 + axis, pl.ds(first, count)],
             send_sem=fwd_send.at[axis],
-            recv_sem=fwd_recv.at[axis, c],
+            recv_sem=fwd_recv.at[axis, c if sem is None else sem],
             device_id=(x3, y3)[axis],
             device_id_type=MESH,
         )
 
+    last = [(CHUNKS - 1, 0, CR // 2, CHUNKS - 1), (CHUNKS - 1, CR // 2, CR // 2, CHUNKS)]
+
     def to_core(h):
         rows = pl.ds(R * h, R)
         return pltpu.make_async_remote_copy(
@@ -99,8 +100,14 @@
 
     def send_ids(p):
         return pltpu.make_async_remote_copy(
-            src_ref=ids, dst_ref=r_ids.at[p], send_sem=ids_send, recv_sem=ids_recv,
+            src_ref=ids, dst_ref=r_ids.at[p], send_sem=ids_send, recv_sem=ids_recv.at[p],
             device_id=partners[p], device_id_type=MESH,
+        )
+
+    def forward_ids(axis):
+        return pltpu.make_async_remote_copy(
+            src_ref=r_ids.at[axis], dst_ref=r_ids.at[2 + axis], send_sem=ids_send, recv_sem=ids_recv.at[2 + axis],
+            device_id=(x3, y3)[axis], device_id_type=MESH,
         )
 
     def send_inv(p):
@@ -116,24 +123,29 @@
         inv_r[rows] = ir
         z[rows] = x * ir
 
-    def launch(c):
-        direct(0, c).start()
-        direct(1, c).start()
+    def launch(*piece):
+        direct(0, *piece).start()
+        direct(1, *piece).start()
 
     loads[0].wait()
     normalise(0, CR)
-    pl.semaphore_wait(barrier, 7)
+    loads[2].wait()
+    for q in range(4):
+        ids[pl.ds(2 * q, 2)] = ids_int[...].astype(F32)
+    pl.semaphore_wait(barrier, 5)
     launch(0)
+    for p in (0, 1, 4):
+        send_ids(p).start()
     normalise(CR, R - CR)
+    for c in range(1, CHUNKS // 2):
+        launch(c)
     to_core(0).start()
     loads[1].wait()
-    loads[2].wait()
-    for q in range(4):
-        ids[pl.ds(2 * q, 2)] = ids_int[...].astype(F32)
-    for p in range(5):
-        send_ids(p).start()
     normalise(R, R)
-    launch(1)
+    for c in range(CHUNKS // 2, CHUNKS - 1):
+        launch(c)
+    for piece in last:
+        launch(*piece)
     to_core(1).start()
 
     zl[...] = (z[...] * LOGIT).astype(BF16)
@@ -165,28 +177,30 @@
     def pair_ids(ref):
         return jnp.concatenate([ref[pl.ds(0, 1)], ref[pl.ds(1, 1)]], axis=1)
 
-    def pass_on(c):
+    def pass_on(*piece):
         for axis in range(2):
-            direct(axis, c).wait_recv()
-            forward(axis, c).start()
-        if isinstance(c, int):
-            launch(c + WINDOW)
-        else:
-            pl.when(c + WINDOW < CHUNKS)(lambda: launch(c + WINDOW))
+            direct(axis, *piece).wait_recv()
+            forward(axis, *piece).start()
 
     own_ids = pair_ids(ids)
     scores(0, z[pl.ds(0, R)], own_ids)
-    launch(2)
+    pass_on(0)
+    for axis in range(2):
+        send_ids(axis).wait_recv()
+        forward_ids(axis).start()
     scores(1, z[pl.ds(R, R)], own_ids)
-    pass_on(0)
-    whole(r_ids, ids_send, ids_recv).wait_recv()
+    pass_on(1)
+    send_ids(4).wait_recv()
     core_ids = pair_ids(r_ids.at[4])
     to_core(0).wait_recv()
     scores(2, core_z[pl.ds(0, R)], core_ids)
-    pass_on(1)
+    pass_on(2)
     to_core(1).wait_recv()
     scores(3, core_z[pl.ds(R, R)], core_ids)
+    pass_on(3)
     gather(0)
+    for axis in range(2):
+        forward_ids(axis).wait_recv()
 
     left = lax.broadcasted_iota(jnp.int32, (8, 128), 1) < 64
 
@@ -202,25 +216,24 @@
         id_rows[pl.ds(2 * q, 1)] = first[q : q + 1]
         id_rows[pl.ds(2 * q + 1, 1)] = second[q : q + 1]
 
-    def arrived(c):
-        for axis in range(2):
-            forward(axis, c).wait_recv()
-
-    def stream_scores(c):
+    def stream_scores(c, pieces):
+        for piece in pieces:
+            for axis in range(2):
+                forward(axis, *piece).wait_recv()
         scores(4 + c, streams[c].reshape(4 * CR, D), id_rows[pl.ds(c % 4, 1)])
 
     def stream_step(c, carry):
-        pass_on(c + 2)
-        arrived(c)
-        stream_scores(c)
+        stream_scores(c, [(c,)])
+        pass_on(c + 4)
         return carry
 
-    lax.fori_loop(0, 4, stream_step, 0)
-    gather(1)
-    lax.fori_loop(4, CHUNKS - 2, stream_step, 0)
-    for c in range(CHUNKS - 2, CHUNKS):
-        arrived(c)
-        stream_scores(c)
+    lax.fori_loop(0, CHUNKS - 5, stream_step, 0)
+    stream_scores(CHUNKS - 5, [(CHUNKS - 5,)])
+    pass_on(*last[0])
+    pass_on(*last[1])
+    for c in range(CHUNKS - 4, CHUNKS - 1):
+        stream_scores(c, [(c,)])
+    stream_scores(CHUNKS - 1, last)
 
     s_hi = den_acc[...].astype(BF16)
     rest = den_acc[...] - s_hi.astype(F32)
@@ -235,6 +248,7 @@
     for p in range(5):
         send_inv(p).start()
 
+    gather(1)
     gather(2)
     centre = jnp.mean(own_inv[0:1], axis=1, keepdims=True)
     inv_col = 1.0 / jnp.sum(den_acc[...], axis=1, keepdims=True)
@@ -271,8 +285,8 @@
         whole(z, direct_send.at[axis], core_recv.at[0]).wait_send()
         whole(z, fwd_send.at[axis], core_recv.at[0]).wait_send()
     whole(z, core_send, core_recv.at[0]).wait_send()
-    whole(r_ids, ids_send, ids_recv).wait_send()
-    whole(r_inv, den_send, den_recv).wait_send()
+    whole(r_ids, ids_send, core_recv.at[0]).wait_send()
+    whole(r_inv, den_send, core_recv.at[0]).wait_send()
 
 
 def finish(z, grad, inv_r, out_one, out_two, result, out_sem):
@@ -324,13 +338,13 @@
             pltpu.VMEM((R, 1), F32),
             dma((3,)),
             dma((2,)),
-            dma((2, CHUNKS)),
+            dma((2, CHUNKS + 1)),
             dma((2,)),
-            dma((2, CHUNKS)),
+            dma((2, CHUNKS + 1)),
             dma,
             dma((2,)),
             dma,
-            dma,
+            dma((5,)),
             dma,
             dma,
         ],

time: 32.5 us -> 31 us (0.954)
  Pallas kernels: 31.6 us -> 30.2 us
    pallas_call x1, Pallas kernels: 30.6 us -> 29.2 us  [on_device(): pl.pallas_call(kernel, out_shape=(pltpu.VMEM((2 * R, D), F32), pltpu.VMEM...]
where the time goes in v4:
time: 31 us; the launch traced here: 30.9 us
  Pallas kernels  30.2 us (97%)
  between operations  0.64 us (2%)
    pallas_call x1, Pallas kernels, on_device(): pl.pallas_call(kernel, out_shape=(pltpu.VMEM((2 * R, D), F32), pltpu.VMEM...  29.2 us
    pallas_call x1, Pallas kernels, on_device(): pl.pallas_call(finish, out_shape=(jax.ShapeDtypeStruct((R, D), F32), jax....  1 us

profile of v4, /device:TPU:6, one launch (start us, length us, event | category | flops | bytes accessed | tf_op | source)
XLA Modules:
  0.0 30.9 jit_solution(12928359695763026257)
XLA Ops:
  0.6 29.2 %shard_map.50 = (f32[512,256]{1,0:T(8,128)S(1)}, f32[512,256]{1,0:T(8,128)S(1)}, f32[512,1]{1,0:T(8,128)S(1)}) custom-call(f32[256,256]{1,0:T(8,128)} %one_hbm.1, f32[256,256]{1,0:T(8,128)} %two_hbm.1, s32[2,128]{1,0:T(2,128)} %bitcast.1), custom_call_target="tpu_custom_call" | custom-call | tf_op jit(solution)/shard_map/pallas_call | solution.py:311
  29.9 1.0 %shard_map.51 = (f32[256,256]{1,0:T(8,128)}, f32[256,256]{1,0:T(8,128)}) custom-call(f32[512,256]{1,0:T(8,128)S(1)} %get-tuple-element.5.z, f32[512,256]{1,0:T(8,128)S(1)} %get-tuple-element.6.grad, f32[512,1]{1,0:T(8,128)S(1)} %get-tuple-element.7.inv_r), custom_call_target="tpu_custom_call" | custom-call | tf_op jit(solution)/shard_map/pallas_call | solution.py:355

commit v5 on v4

--- a/solution.py
+++ b/solution.py
@@ -38,7 +38,7 @@
 
 def kernel(
     one_hbm, two_hbm, ids_hbm, z, grad, inv_r,
-    raw, zl, core_z, streams, keys_all, e_all, acc, key_sum, den_acc, id_col, ids_int, ids, r_ids, id_rows,
+    raw, zl_hi, zl_lo, core_z, streams, k_hi, k_lo, e_hi, e_lo, acc, den_acc, id_col, ids_int, ids, r_ids, id_rows,
     inv_row, r_inv, inv_rows, diag,
     load_sem, direct_send, direct_recv, fwd_send, fwd_recv, core_send, core_recv, ids_send, ids_recv, den_send, den_recv,
 ):
@@ -112,7 +112,7 @@
 
     def send_inv(p):
         return pltpu.make_async_remote_copy(
-            src_ref=inv_row, dst_ref=r_inv.at[p], send_sem=den_send, recv_sem=den_recv,
+            src_ref=inv_row, dst_ref=r_inv.at[p], send_sem=den_send, recv_sem=den_recv.at[p // 4],
             device_id=partners[p], device_id_type=MESH,
         )
 
@@ -137,41 +137,48 @@
     for p in (0, 1, 4):
         send_ids(p).start()
     normalise(CR, R - CR)
-    for c in range(1, CHUNKS // 2):
+    launch(1)
+    to_core(0).start()
+    for c in range(2, CHUNKS // 2):
         launch(c)
-    to_core(0).start()
     loads[1].wait()
     normalise(R, R)
-    for c in range(CHUNKS // 2, CHUNKS - 1):
+    launch(CHUNKS // 2)
+    to_core(1).start()
+    for c in range(CHUNKS // 2 + 1, CHUNKS - 1):
         launch(c)
     for piece in last:
         launch(*piece)
-    to_core(1).start()
-
-    zl[...] = (z[...] * LOGIT).astype(BF16)
+
+    hi, lo = split(z[...] * LOGIT)
+    zl_hi[...] = hi
+    zl_lo[...] = lo
     d = jnp.exp2(LOGIT * jnp.sum(z[pl.ds(0, R)] * z[pl.ds(R, R)], axis=1, keepdims=True))
     diag[...] = d
     lane = lax.broadcasted_iota(jnp.int32, (R, 128), 1)
     start = jnp.where(lane == 0, d, 0.0)
     den_acc[pl.ds(0, R)] = start
     den_acc[pl.ds(R, R)] = start
-    key_sum[...] = jnp.zeros_like(key_sum)
     for q in range(2):
         id_col[pl.ds(128 * q, 128)] = jnp.broadcast_to(ids[pl.ds(q, 1)], (128, 128)).T
 
-    def scores(slot, keys, key_ids):
-        place = pl.ds(pl.multiple_of(256 * slot, 256), 256)
-        narrow = keys.astype(BF16)
-        keys_all[place] = narrow
-        key_sum[...] += jnp.sum(keys.reshape(32, 8, D), axis=0)
-        keep = jnp.concatenate([id_col[...], id_col[...]], axis=1) != key_ids
-        e = jnp.where(jnp.concatenate([keep, keep], axis=0), jnp.exp2(dot_t(zl[...], narrow)), 0.0)
-        den_acc[...] += e[:, :128] + e[:, 128:]
-        e_all[:, place] = (e - 1.0).astype(BF16)
+    def scores(lane, keys, key_ids):
+        width = keys.shape[0]
+        place = pl.ds(lane, width)
+        khi, klo = split(keys)
+        k_hi[place] = khi
+        k_lo[place] = klo
+        keep = jnp.concatenate([id_col[...]] * (width // 128), axis=1) != key_ids
+        s = dot_t(zl_hi[...], khi) + dot_t(zl_hi[...], klo) + dot_t(zl_lo[...], khi)
+        e = jnp.where(jnp.concatenate([keep, keep], axis=0), jnp.exp2(s), 0.0)
+        den_acc[...] += sum(e[:, q : q + 128] for q in range(0, width, 128))
+        ehi, elo = split(e)
+        e_hi[:, place] = ehi
+        e_lo[:, place] = elo
 
     def gather(group):
         place = pl.ds(1024 * group, 1024)
-        part = dot(e_all[:, place], keys_all[place])
+        part = dot(e_hi[:, place], k_hi[place]) + dot(e_hi[:, place], k_lo[place]) + dot(e_lo[:, place], k_hi[place])
         acc[...] = part if group == 0 else acc[...] + part
 
     def pair_ids(ref):
@@ -184,19 +191,19 @@
 
     own_ids = pair_ids(ids)
     scores(0, z[pl.ds(0, R)], own_ids)
+    scores(R, z[pl.ds(R, R)], own_ids)
     pass_on(0)
     for axis in range(2):
         send_ids(axis).wait_recv()
         forward_ids(axis).start()
-    scores(1, z[pl.ds(R, R)], own_ids)
-    pass_on(1)
     send_ids(4).wait_recv()
     core_ids = pair_ids(r_ids.at[4])
+    pass_on(1)
     to_core(0).wait_recv()
-    scores(2, core_z[pl.ds(0, R)], core_ids)
+    scores(2 * R, core_z[pl.ds(0, R)], core_ids)
     pass_on(2)
     to_core(1).wait_recv()
-    scores(3, core_z[pl.ds(R, R)], core_ids)
+    scores(3 * R, core_z[pl.ds(R, R)], core_ids)
     pass_on(3)
     gather(0)
     for axis in range(2):
@@ -216,47 +223,59 @@
         id_rows[pl.ds(2 * q, 1)] = first[q : q + 1]
         id_rows[pl.ds(2 * q + 1, 1)] = second[q : q + 1]
 
-    def stream_scores(c, pieces):
-        for piece in pieces:
-            for axis in range(2):
-                forward(axis, *piece).wait_recv()
-        scores(4 + c, streams[c].reshape(4 * CR, D), id_rows[pl.ds(c % 4, 1)])
+    def stream_scores(c):
+        for axis in range(2):
+            forward(axis, c).wait_recv()
+        lane = pl.multiple_of(4 * R + 4 * CR * c, 4 * CR)
+        scores(lane, streams[c].reshape(4 * CR, D), id_rows[pl.ds(c % 4, 1)])
 
     def stream_step(c, carry):
-        stream_scores(c, [(c,)])
+        stream_scores(c)
         pass_on(c + 4)
         return carry
 
     lax.fori_loop(0, CHUNKS - 5, stream_step, 0)
-    stream_scores(CHUNKS - 5, [(CHUNKS - 5,)])
+    stream_scores(CHUNKS - 5)
     pass_on(*last[0])
     pass_on(*last[1])
-    for c in range(CHUNKS - 4, CHUNKS - 1):
-        stream_scores(c, [(c,)])
-    stream_scores(CHUNKS - 1, last)
+    end = CHUNKS - 1
+    end_lane = 4 * R + 4 * CR * end
+    end_ids = id_rows[pl.ds(end % 4, 1)]
+    scores(end_lane, streams[end, pl.ds(0, 2)].reshape(2 * CR, D), end_ids[:, :128])
+    gather(1)
+    for c in range(CHUNKS - 4, end):
+        stream_scores(c)
 
     s_hi = den_acc[...].astype(BF16)
     rest = den_acc[...] - s_hi.astype(F32)
     s_mid, s_lo = split(rest)
     ones = jnp.ones((8, 128), BF16)
+    inv_row[...] = jnp.zeros_like(inv_row)
     sums = dot_t(ones, s_hi) + dot_t(ones, s_mid) + dot_t(ones, s_lo)
-    own_inv = 1.0 / sums
+    end_keep = jnp.concatenate([jnp.broadcast_to(end_ids[:, 128:], (128, 128)).T] * 4, axis=1) != jnp.concatenate(
+        [own_ids, own_ids], axis=1
+    )
+
+    for piece in last:
+        for axis in range(2):
+            forward(axis, *piece).wait_recv()
+    khi, klo = split(streams[end, pl.ds(2, 2)].reshape(2 * CR, D))
+    turned = dot_t(khi, zl_hi[...]) + dot_t(klo, zl_hi[...]) + dot_t(khi, zl_lo[...])
+    turned = jnp.where(end_keep, jnp.exp2(turned), 0.0)
+    own_inv = 1.0 / (sums[0:1] + jnp.sum(turned, axis=0, keepdims=True))
     for q in range(4):
-        inv_row[pl.ds(q, 1)] = own_inv[0:1, 128 * q : 128 * (q + 1)]
-    for q in range(4):
-        inv_row[pl.ds(4 + q, 1)] = own_inv[0:1, 128 * q : 128 * (q + 1)]
+        inv_row[pl.ds(q, 1)] = own_inv[:, 128 * q : 128 * (q + 1)]
     for p in range(5):
         send_inv(p).start()
 
-    gather(1)
+    scores(end_lane + 128, streams[end, pl.ds(2, 2)].reshape(2 * CR, D), end_ids[:, 128:])
     gather(2)
-    centre = jnp.mean(own_inv[0:1], axis=1, keepdims=True)
+    centre = jnp.mean(own_inv, axis=1, keepdims=True)
     inv_col = 1.0 / jnp.sum(den_acc[...], axis=1, keepdims=True)
     coef = diag[...] * (inv_col[:R] + inv_col[R:]) - 1.0 / TAU
     for h in range(2):
         rows, others = pl.ds(R * h, R), pl.ds(R * (1 - h), R)
-        total = acc[rows] + jnp.sum(key_sum[...], axis=0, keepdims=True)
-        acc[rows] = (inv_col[R * h : R * (h + 1)] + centre) * total + coef * z[others]
+        acc[rows] = (inv_col[R * h : R * (h + 1)] + centre) * acc[rows] + coef * z[others]
 
     def spread(slot, row, lane, values):
         inv_rows[0:1, pl.ds(256 * slot + lane, values.shape[1])] = values[row : row + 1] - centre
@@ -264,22 +283,22 @@
     def weighted(first, count):
         place = pl.ds(256 * first, 256 * count)
         off = jnp.broadcast_to(inv_rows[0:1, place], (16, 256 * count)).astype(BF16)[None]
-        e = e_all[:, place].reshape(2 * R // 16, 16, 256 * count)
-        return dot((e * off + off).reshape(2 * R, 256 * count), keys_all[place])
-
-    own = inv_row[...]
+        e = e_hi[:, place].reshape(2 * R // 16, 16, 256 * count)
+        return dot((e * off).reshape(2 * R, 256 * count), k_hi[place])
+
+    send_inv(4).wait_recv()
+    own, other = inv_row[...], r_inv[4]
     for q in range(4):
         spread(q // 2, q, 128 * (q % 2), own)
-    acc[...] += weighted(0, 2)
-
-    whole(r_inv, den_send, den_recv).wait_recv()
+        spread(2 + q // 2, q, 128 * (q % 2), other)
+    acc[...] += weighted(0, 4)
+
+    whole(r_inv.at[pl.ds(0, 4)], den_send, den_recv.at[0]).wait_recv()
     first, second = mixed(r_inv)
-    other = r_inv[4]
     for q in range(4):
-        spread(2 + q // 2, q, 128 * (q % 2), other)
         spread(4 + 2 * q, q, 0, first)
         spread(5 + 2 * q, q, 0, second)
-    grad[...] = acc[...] + weighted(2, STEPS - 2)
+    grad[...] = acc[...] + weighted(4, STEPS - 4)
 
     for axis in range(2):
         whole(z, direct_send.at[axis], core_recv.at[0]).wait_send()
@@ -320,12 +339,14 @@
         scratch_shapes=[
             pltpu.VMEM((2 * R, D), F32),
             pltpu.VMEM((2 * R, D), BF16),
+            pltpu.VMEM((2 * R, D), BF16),
             pltpu.VMEM((2 * R, D), F32),
             pltpu.VMEM((CHUNKS, 4, CR, D), F32),
             pltpu.VMEM((256 * STEPS, D), BF16),
+            pltpu.VMEM((256 * STEPS, D), BF16),
             pltpu.VMEM((2 * R, 256 * STEPS), BF16),
-            pltpu.VMEM((2 * R, D), F32),
-            pltpu.VMEM((8, D), F32),
+            pltpu.VMEM((2 * R, 256 * STEPS), BF16),
+            pltpu.VMEM((2 * R, D), F32),
             pltpu.VMEM((2 * R, 128), F32),
             pltpu.VMEM((R, 128), F32),
             pltpu.VMEM((2, 128), jnp.int32),
@@ -346,7 +367,7 @@
             dma,
             dma((5,)),
             dma,
-            dma,
+            dma((2,)),
         ],
         compiler_params=pltpu.CompilerParams(
             collective_id=0, has_side_effects=True, vmem_limit_bytes=32 * 1024 * 1024

time: 31 us -> 31.6 us (1.019)
  Pallas kernels: 30.2 us -> 30.7 us
    pallas_call x1, Pallas kernels: 29.2 us -> 29.7 us  [on_device(): pl.pallas_call(kernel, out_shape=(pltpu.VMEM((2 * R, D), F32), pltpu.VMEM...]
where the time goes in v5:
time: 31.6 us; the launch traced here: 31.3 us
  Pallas kernels  30.7 us (97%)
  between operations  0.64 us (2%)
    pallas_call x1, Pallas kernels, on_device(): pl.pallas_call(kernel, out_shape=(pltpu.VMEM((2 * R, D), F32), pltpu.VMEM...  29.7 us
    pallas_call x1, Pallas kernels, on_device(): pl.pallas_call(finish, out_shape=(jax.ShapeDtypeStruct((R, D), F32), jax....  1 us

profile of v5, /device:TPU:6, one launch (start us, length us, event | category | flops | bytes accessed | tf_op | source)
XLA Modules:
  0.0 31.3 jit_solution(11947415109403301208)
XLA Ops:
  0.6 29.7 %shard_map.50 = (f32[512,256]{1,0:T(8,128)S(1)}, f32[512,256]{1,0:T(8,128)S(1)}, f32[512,1]{1,0:T(8,128)S(1)}) custom-call(f32[256,256]{1,0:T(8,128)} %one_hbm.1, f32[256,256]{1,0:T(8,128)} %two_hbm.1, s32[2,128]{1,0:T(2,128)} %bitcast.1), custom_call_target="tpu_custom_call" | custom-call | tf_op jit(solution)/shard_map/pallas_call | solution.py:330
  30.3 1.0 %shard_map.51 = (f32[256,256]{1,0:T(8,128)}, f32[256,256]{1,0:T(8,128)}) custom-call(f32[512,256]{1,0:T(8,128)S(1)} %get-tuple-element.5.z, f32[512,256]{1,0:T(8,128)S(1)} %get-tuple-element.6.grad, f32[512,1]{1,0:T(8,128)S(1)} %get-tuple-element.7.inv_r), custom_call_target="tpu_custom_call" | custom-call | tf_op jit(solution)/shard_map/pallas_call | solution.py:376

commit v6 on v5

--- a/solution.py
+++ b/solution.py
@@ -37,19 +37,21 @@
 
 
 def kernel(
-    one_hbm, two_hbm, ids_hbm, z, grad, inv_r,
-    raw, zl_hi, zl_lo, core_z, streams, k_hi, k_lo, e_hi, e_lo, acc, den_acc, id_col, ids_int, ids, r_ids, id_rows,
-    inv_row, r_inv, inv_rows, diag,
+    one_hbm, two_hbm, ids_hbm, z, acc, inv_r, k_hi, e_hi, inv_rows,
+    raw, zl_hi, zl_lo, core_z, streams, k_lo, e_lo, den_acc, id_col, ids_int, ids, r_ids, id_rows,
+    inv_row, r_inv, diag,
     load_sem, direct_send, direct_recv, fwd_send, fwd_recv, core_send, core_recv, ids_send, ids_recv, den_send, den_recv,
 ):
     blk, grp = lax.axis_index("blk"), lax.axis_index("grp")
-    x1 = (flip(blk, 2), grp)
-    x3 = (flip(blk, 2), flip(grp, 1))
-    y1 = (blk, flip(grp, 2))
-    y3 = (blk, flip(flip(grp, 2), 4))
     core = (flip(blk, 1), grp)
-    x2 = (blk, flip(grp, 1))
-    y2 = (blk, flip(grp, 4))
+    side = blk % 2
+
+    def turn(x, y):
+        return tuple(p + side * (q - p) for p, q in zip(x, y)), tuple(q + side * (p - q) for p, q in zip(x, y))
+
+    x1, y1 = turn((flip(blk, 2), grp), (blk, flip(grp, 2)))
+    x3, y3 = turn((flip(blk, 2), flip(grp, 1)), (blk, flip(flip(grp, 2), 4)))
+    x2, y2 = turn((blk, flip(grp, 1)), (blk, flip(grp, 4)))
     partners = (x1, y1, x2, y2, core)
 
     barrier = pltpu.get_barrier_semaphore()
@@ -84,6 +86,7 @@
             device_id_type=MESH,
         )
 
+    opening = [(0, 0, CR // 2, CHUNKS + 1), (0, CR // 2, CR // 2, 0)]
     last = [(CHUNKS - 1, 0, CR // 2, CHUNKS - 1), (CHUNKS - 1, CR // 2, CR // 2, CHUNKS)]
 
     def to_core(h):
@@ -133,7 +136,8 @@
     for q in range(4):
         ids[pl.ds(2 * q, 2)] = ids_int[...].astype(F32)
     pl.semaphore_wait(barrier, 5)
-    launch(0)
+    for piece in opening:
+        launch(*piece)
     for p in (0, 1, 4):
         send_ids(p).start()
     normalise(CR, R - CR)
@@ -192,7 +196,8 @@
     own_ids = pair_ids(ids)
     scores(0, z[pl.ds(0, R)], own_ids)
     scores(R, z[pl.ds(R, R)], own_ids)
-    pass_on(0)
+    for piece in opening:
+        pass_on(*piece)
     for axis in range(2):
         send_ids(axis).wait_recv()
         forward_ids(axis).start()
@@ -223,9 +228,10 @@
         id_rows[pl.ds(2 * q, 1)] = first[q : q + 1]
         id_rows[pl.ds(2 * q + 1, 1)] = second[q : q + 1]
 
-    def stream_scores(c):
-        for axis in range(2):
-            forward(axis, c).wait_recv()
+    def stream_scores(c, pieces=None):
+        for piece in pieces or [(c,)]:
+            for axis in range(2):
+                forward(axis, *piece).wait_recv()
         lane = pl.multiple_of(4 * R + 4 * CR * c, 4 * CR)
         scores(lane, streams[c].reshape(4 * CR, D), id_rows[pl.ds(c % 4, 1)])
 
@@ -234,7 +240,9 @@
         pass_on(c + 4)
         return carry
 
-    lax.fori_loop(0, CHUNKS - 5, stream_step, 0)
+    stream_scores(0, opening)
+    pass_on(4)
+    lax.fori_loop(1, CHUNKS - 5, stream_step, 0)
     stream_scores(CHUNKS - 5)
     pass_on(*last[0])
     pass_on(*last[1])
@@ -280,25 +288,18 @@
     def spread(slot, row, lane, values):
         inv_rows[0:1, pl.ds(256 * slot + lane, values.shape[1])] = values[row : row + 1] - centre
 
-    def weighted(first, count):
-        place = pl.ds(256 * first, 256 * count)
-        off = jnp.broadcast_to(inv_rows[0:1, place], (16, 256 * count)).astype(BF16)[None]
-        e = e_hi[:, place].reshape(2 * R // 16, 16, 256 * count)
-        return dot((e * off).reshape(2 * R, 256 * count), k_hi[place])
-
     send_inv(4).wait_recv()
     own, other = inv_row[...], r_inv[4]
     for q in range(4):
         spread(q // 2, q, 128 * (q % 2), own)
         spread(2 + q // 2, q, 128 * (q % 2), other)
-    acc[...] += weighted(0, 4)
+    acc[...] += weighted(e_hi, k_hi, inv_rows, pl.ds(0, 2 * R), pl.ds(0, 4 * R))
 
     whole(r_inv.at[pl.ds(0, 4)], den_send, den_recv.at[0]).wait_recv()
     first, second = mixed(r_inv)
     for q in range(4):
         spread(4 + 2 * q, q, 0, first)
         spread(5 + 2 * q, q, 0, second)
-    grad[...] = acc[...] + weighted(4, STEPS - 4)
 
     for axis in range(2):
         whole(z, direct_send.at[axis], core_recv.at[0]).wait_send()
@@ -308,15 +309,20 @@
     whole(r_inv, den_send, core_recv.at[0]).wait_send()
 
 
-def finish(z, grad, inv_r, out_one, out_two, result, out_sem):
+def weighted(e_hi, k_hi, inv_rows, rows, keys):
+    off = jnp.broadcast_to(inv_rows[0:1, keys], (16, keys.size)).astype(BF16)[None]
+    e = e_hi[rows, keys].reshape(rows.size // 16, 16, keys.size)
+    return dot((e * off).reshape(rows.size, keys.size), k_hi[keys])
+
+
+def finish(z, acc, inv_r, k_hi, e_hi, inv_rows, out_one, out_two, result, out_sem):
     outs = []
-    for c in range(4):
-        rows = pl.ds(128 * c, 128)
-        g, own = grad[rows], z[rows]
+    for h in range(2):
+        rows = pl.ds(R * h, R)
+        g = acc[rows] + weighted(e_hi, k_hi, inv_rows, rows, pl.ds(4 * R, (STEPS - 4) * 256))
+        own = z[rows]
         result[rows] = (g - own * jnp.sum(own * g, axis=1, keepdims=True)) * inv_r[rows]
-        copy = pltpu.make_async_copy(
-            result.at[rows], (out_one, out_two)[c // 2].at[pl.ds(128 * (c % 2), 128)], out_sem.at[c]
-        )
+        copy = pltpu.make_async_copy(result.at[rows], (out_one, out_two)[h], out_sem.at[h])
         copy.start()
         outs.append(copy)
     for copy in outs:
@@ -333,9 +339,12 @@
             pltpu.VMEM((2 * R, D), F32),
             pltpu.VMEM((2 * R, D), F32),
             pltpu.VMEM((2 * R, 1), F32),
+            pltpu.VMEM((256 * STEPS, D), BF16),
+            pltpu.VMEM((2 * R, 256 * STEPS), BF16),
+            pltpu.VMEM((8, 256 * STEPS), F32),
         ),
         in_specs=[hbm] * 3,
-        out_specs=(vmem,) * 3,
+        out_specs=(vmem,) * 6,
         scratch_shapes=[
             pltpu.VMEM((2 * R, D), F32),
             pltpu.VMEM((2 * R, D), BF16),
@@ -343,10 +352,7 @@
             pltpu.VMEM((2 * R, D), F32),
             pltpu.VMEM((CHUNKS, 4, CR, D), F32),
             pltpu.VMEM((256 * STEPS, D), BF16),
-            pltpu.VMEM((256 * STEPS, D), BF16),
             pltpu.VMEM((2 * R, 256 * STEPS), BF16),
-            pltpu.VMEM((2 * R, 256 * STEPS), BF16),
-            pltpu.VMEM((2 * R, D), F32),
             pltpu.VMEM((2 * R, 128), F32),
             pltpu.VMEM((R, 128), F32),
             pltpu.VMEM((2, 128), jnp.int32),
@@ -355,13 +361,12 @@
             pltpu.VMEM((8, 256), F32),
             pltpu.VMEM((8, 128), F32),
             pltpu.VMEM((5, 8, 128), F32),
-            pltpu.VMEM((8, 256 * STEPS), F32),
             pltpu.VMEM((R, 1), F32),
             dma((3,)),
             dma((2,)),
-            dma((2, CHUNKS + 1)),
+            dma((2, CHUNKS + 2)),
             dma((2,)),
-            dma((2, CHUNKS + 1)),
+            dma((2, CHUNKS + 2)),
             dma,
             dma((2,)),
             dma,
@@ -376,10 +381,10 @@
     return pl.pallas_call(
         finish,
         out_shape=(jax.ShapeDtypeStruct((R, D), F32), jax.ShapeDtypeStruct((R, D), F32)),
-        in_specs=[vmem] * 3,
+        in_specs=[vmem] * 6,
         out_specs=(hbm, hbm),
-        scratch_shapes=[pltpu.VMEM((2 * R, D), F32), dma((4,))],
-        compiler_params=pltpu.CompilerParams(vmem_limit_bytes=4 * 1024 * 1024),
+        scratch_shapes=[pltpu.VMEM((2 * R, D), F32), dma((2,))],
+        compiler_params=pltpu.CompilerParams(vmem_limit_bytes=8 * 1024 * 1024),
     )(*middle)
 
 

time: 31.6 us -> 30.7 us (0.972)
  Pallas kernels: 30.7 us -> 29.8 us
    pallas_call x1, Pallas kernels: 29.7 us -> 28.2 us  [on_device(): pl.pallas_call(kernel, out_shape=(pltpu.VMEM((2 * R, D), F32), pltpu.VMEM...]
    pallas_call x1, Pallas kernels: 1 us -> 1.61 us  [on_device(): pl.pallas_call(finish, out_shape=(jax.ShapeDtypeStruct((R, D), F32), jax....]
where the time goes in v6:
time: 30.7 us; the launch traced here: 30.5 us
  Pallas kernels  29.8 us (97%)
  between operations  0.64 us (2%)
    pallas_call x1, Pallas kernels, on_device(): pl.pallas_call(kernel, out_shape=(pltpu.VMEM((2 * R, D), F32), pltpu.VMEM...  28.2 us
    pallas_call x1, Pallas kernels, on_device(): pl.pallas_call(finish, out_shape=(jax.ShapeDtypeStruct((R, D), F32), jax....  1.61 us

profile of v6, /device:TPU:6, one launch (start us, length us, event | category | flops | bytes accessed | tf_op | source)
XLA Modules:
  0.0 30.5 jit_solution(15062029093988780413)
XLA Ops:
  0.6 28.2 %shard_map.50 = (f32[512,256]{1,0:T(8,128)S(1)}, f32[512,256]{1,0:T(8,128)S(1)}, f32[512,1]{1,0:T(8,128)S(1)}, bf16[3072,256]{1,0:T(8,128)(2,1)S(1)}, bf16[512,3...) custom-call(f32[256,256]{1,0:T(8,128)} %one_hbm.1, f32[256,256]{1,0:T(8,128)} %two_hbm.1, s32[2,128]{1,0:T(2,128)} %bitcast.1), custom_call_target="tpu_custom_call" | custom-call | tf_op jit(solution)/shard_map/pallas_call | solution.py:336
  28.8 1.6 %shard_map.51 = (f32[256,256]{1,0:T(8,128)}, f32[256,256]{1,0:T(8,128)}) custom-call(f32[512,256]{1,0:T(8,128)S(1)} %get-tuple-element.8.z, f32[512,256]{1,0:T(8,128)S(1)} %get-tuple-element.9.acc, f32[512,1]{1,0:T(8,128)S(1)} %get-tuple-element.10.inv_r, bf16[3072,256]{1,0:T(8,128)(2,1)S(1)} %get-tuple-element.11.k_hi, ...), custom_call_target="tpu_custom_call" | custom-call | tf_op jit(solution)/shard_map/pallas_call | solution.py:381

commit v7 on v6

--- a/solution.py
+++ b/solution.py
@@ -67,8 +67,12 @@
         copy.start()
 
     def direct(axis, c, first=0, count=CR, sem=None):
-        return pltpu.make_async_remote_copy(
-            src_ref=z.at[pl.ds(CR * c + first, count)],
+        source = raw.at[pl.ds(CR * c + first, count)]
+        if isinstance(c, int):
+            view, at = (one_hbm, two_hbm)[c // (CHUNKS // 2)], CR * (c % (CHUNKS // 2))
+            source = view.at[pl.ds(at + first, count)]
+        return pltpu.make_async_remote_copy(
+            src_ref=source,
             dst_ref=streams.at[c, axis, pl.ds(first, count)],
             send_sem=direct_send.at[axis],
             recv_sem=direct_recv.at[axis, c if sem is None else sem],
@@ -92,7 +96,7 @@
     def to_core(h):
         rows = pl.ds(R * h, R)
         return pltpu.make_async_remote_copy(
-            src_ref=z.at[rows], dst_ref=core_z.at[rows], send_sem=core_send, recv_sem=core_recv.at[h],
+            src_ref=(one_hbm, two_hbm)[h], dst_ref=core_z.at[rows], send_sem=core_send, recv_sem=core_recv.at[h],
             device_id=core, device_id_type=MESH,
         )
 
@@ -119,40 +123,38 @@
             device_id=partners[p], device_id_type=MESH,
         )
 
-    def normalise(first, count):
-        rows = pl.ds(first, count)
-        x = raw[rows]
-        ir = lax.rsqrt(jnp.sum(x * x, axis=1, keepdims=True) + 1e-06)
-        inv_r[rows] = ir
-        z[rows] = x * ir
+    def inverse_radius(x):
+        return lax.rsqrt(jnp.sum(x * x, axis=1, keepdims=True) + 1e-06)
+
+    def unit(x):
+        return x * inverse_radius(x)
 
     def launch(*piece):
         direct(0, *piece).start()
         direct(1, *piece).start()
 
-    loads[0].wait()
-    normalise(0, CR)
+    pl.semaphore_wait(barrier, 5)
+    for piece in opening:
+        launch(*piece)
+    launch(1)
+    for h in range(2):
+        to_core(h).start()
     loads[2].wait()
     for q in range(4):
         ids[pl.ds(2 * q, 2)] = ids_int[...].astype(F32)
-    pl.semaphore_wait(barrier, 5)
-    for piece in opening:
-        launch(*piece)
     for p in (0, 1, 4):
         send_ids(p).start()
-    normalise(CR, R - CR)
-    launch(1)
-    to_core(0).start()
-    for c in range(2, CHUNKS // 2):
-        launch(c)
-    loads[1].wait()
-    normalise(R, R)
-    launch(CHUNKS // 2)
-    to_core(1).start()
-    for c in range(CHUNKS // 2 + 1, CHUNKS - 1):
+    for c in range(2, CHUNKS - 1):
         launch(c)
     for piece in last:
         launch(*piece)
+    for h in range(2):
+        rows = pl.ds(R * h, R)
+        loads[h].wait()
+        x = raw[rows]
+        ir = inverse_radius(x)
+        inv_r[rows] = ir
+        z[rows] = x * ir
 
     hi, lo = split(z[...] * LOGIT)
     zl_hi[...] = hi
@@ -205,10 +207,10 @@
     core_ids = pair_ids(r_ids.at[4])
     pass_on(1)
     to_core(0).wait_recv()
-    scores(2 * R, core_z[pl.ds(0, R)], core_ids)
+    scores(2 * R, unit(core_z[pl.ds(0, R)]), core_ids)
     pass_on(2)
     to_core(1).wait_recv()
-    scores(3 * R, core_z[pl.ds(R, R)], core_ids)
+    scores(3 * R, unit(core_z[pl.ds(R, R)]), core_ids)
     pass_on(3)
     gather(0)
     for axis in range(2):
@@ -233,7 +235,7 @@
             for axis in range(2):
                 forward(axis, *piece).wait_recv()
         lane = pl.multiple_of(4 * R + 4 * CR * c, 4 * CR)
-        scores(lane, streams[c].reshape(4 * CR, D), id_rows[pl.ds(c % 4, 1)])
+        scores(lane, unit(streams[c].reshape(4 * CR, D)), id_rows[pl.ds(c % 4, 1)])
 
     def stream_step(c, carry):
         stream_scores(c)
@@ -249,7 +251,7 @@
     end = CHUNKS - 1
     end_lane = 4 * R + 4 * CR * end
     end_ids = id_rows[pl.ds(end % 4, 1)]
-    scores(end_lane, streams[end, pl.ds(0, 2)].reshape(2 * CR, D), end_ids[:, :128])
+    scores(end_lane, unit(streams[end, pl.ds(0, 2)].reshape(2 * CR, D)), end_ids[:, :128])
     gather(1)
     for c in range(CHUNKS - 4, end):
         stream_scores(c)
@@ -267,16 +269,17 @@
     for piece in last:
         for axis in range(2):
             forward(axis, *piece).wait_recv()
-    khi, klo = split(streams[end, pl.ds(2, 2)].reshape(2 * CR, D))
+    end_keys = unit(streams[end, pl.ds(2, 2)].reshape(2 * CR, D))
+    khi, klo = split(end_keys)
     turned = dot_t(khi, zl_hi[...]) + dot_t(klo, zl_hi[...]) + dot_t(khi, zl_lo[...])
     turned = jnp.where(end_keep, jnp.exp2(turned), 0.0)
     own_inv = 1.0 / (sums[0:1] + jnp.sum(turned, axis=0, keepdims=True))
     for q in range(4):
         inv_row[pl.ds(q, 1)] = own_inv[:, 128 * q : 128 * (q + 1)]
-    for p in range(5):
+    for p in (2, 3, 0, 1, 4):
         send_inv(p).start()
 
-    scores(end_lane + 128, streams[end, pl.ds(2, 2)].reshape(2 * CR, D), end_ids[:, 128:])
+    scores(end_lane + 128, end_keys, end_ids[:, 128:])
     gather(2)
     centre = jnp.mean(own_inv, axis=1, keepdims=True)
     inv_col = 1.0 / jnp.sum(den_acc[...], axis=1, keepdims=True)

time: 30.7 us -> 31.5 us (1.026)
  Pallas kernels: 29.8 us -> 30.7 us
    pallas_call x1, Pallas kernels: 28.2 us -> 29.1 us  [on_device(): pl.pallas_call(kernel, out_shape=(pltpu.VMEM((2 * R, D), F32), pltpu.VMEM...]
where the time goes in v7:
time: 31.5 us; the launch traced here: 31.4 us
  Pallas kernels  30.7 us (97%)
  between operations  0.64 us (2%)
    pallas_call x1, Pallas kernels, on_device(): pl.pallas_call(kernel, out_shape=(pltpu.VMEM((2 * R, D), F32), pltpu.VMEM...  29.1 us
    pallas_call x1, Pallas kernels, on_device(): pl.pallas_call(finish, out_shape=(jax.ShapeDtypeStruct((R, D), F32), jax....  1.61 us

profile of v7, /device:TPU:6, one launch (start us, length us, event | category | flops | bytes accessed | tf_op | source)
XLA Modules:
  0.0 31.4 jit_solution(10974342077362032575)
XLA Ops:
  0.6 29.1 %shard_map.50 = (f32[512,256]{1,0:T(8,128)S(1)}, f32[512,256]{1,0:T(8,128)S(1)}, f32[512,1]{1,0:T(8,128)S(1)}, bf16[3072,256]{1,0:T(8,128)(2,1)S(1)}, bf16[512,3...) custom-call(f32[256,256]{1,0:T(8,128)} %one_hbm.1, f32[256,256]{1,0:T(8,128)} %two_hbm.1, s32[2,128]{1,0:T(2,128)} %bitcast.1), custom_call_target="tpu_custom_call" | custom-call | tf_op jit(solution)/shard_map/pallas_call | solution.py:339
  29.7 1.6 %shard_map.51 = (f32[256,256]{1,0:T(8,128)}, f32[256,256]{1,0:T(8,128)}) custom-call(f32[512,256]{1,0:T(8,128)S(1)} %get-tuple-element.8.z, f32[512,256]{1,0:T(8,128)S(1)} %get-tuple-element.9.acc, f32[512,1]{1,0:T(8,128)S(1)} %get-tuple-element.10.inv_r, bf16[3072,256]{1,0:T(8,128)(2,1)S(1)} %get-tuple-element.11.k_hi, ...), custom_call_target="tpu_custom_call" | custom-call | tf_op jit(solution)/shard_map/pallas_call | solution.py:384

commit v8 on v6

--- a/solution.py
+++ b/solution.py
@@ -210,7 +210,6 @@
     to_core(1).wait_recv()
     scores(3 * R, core_z[pl.ds(R, R)], core_ids)
     pass_on(3)
-    gather(0)
     for axis in range(2):
         forward_ids(axis).wait_recv()
 
@@ -250,7 +249,6 @@
     end_lane = 4 * R + 4 * CR * end
     end_ids = id_rows[pl.ds(end % 4, 1)]
     scores(end_lane, streams[end, pl.ds(0, 2)].reshape(2 * CR, D), end_ids[:, :128])
-    gather(1)
     for c in range(CHUNKS - 4, end):
         stream_scores(c)
 
@@ -273,11 +271,12 @@
     own_inv = 1.0 / (sums[0:1] + jnp.sum(turned, axis=0, keepdims=True))
     for q in range(4):
         inv_row[pl.ds(q, 1)] = own_inv[:, 128 * q : 128 * (q + 1)]
-    for p in range(5):
+    for p in (2, 3, 0, 1, 4):
         send_inv(p).start()
 
     scores(end_lane + 128, streams[end, pl.ds(2, 2)].reshape(2 * CR, D), end_ids[:, 128:])
-    gather(2)
+    for group in range(STEPS // 4):
+        gather(group)
     centre = jnp.mean(own_inv, axis=1, keepdims=True)
     inv_col = 1.0 / jnp.sum(den_acc[...], axis=1, keepdims=True)
     coef = diag[...] * (inv_col[:R] + inv_col[R:]) - 1.0 / TAU

time: 30.7 us -> 32 us (1.042)
  the two profiles are of different devices: /device:TPU:6 before, /device:TPU:2 now
where the time goes in v8:
time: 32 us; the launch traced here: 31.9 us
  Pallas kernels  31.2 us (98%)
  between operations  0.64 us (2%)
    pallas_call x1, Pallas kernels, on_device(): pl.pallas_call(kernel, out_shape=(pltpu.VMEM((2 * R, D), F32), pltpu.VMEM...  29.6 us
    pallas_call x1, Pallas kernels, on_device(): pl.pallas_call(finish, out_shape=(jax.ShapeDtypeStruct((R, D), F32), jax....  1.6 us

profile of v8, /device:TPU:2, one launch (start us, length us, event | category | flops | bytes accessed | tf_op | source)
XLA Modules:
  0.0 31.9 jit_solution(7530590447925231252)
XLA Ops:
  0.6 29.6 %shard_map.50 = (f32[512,256]{1,0:T(8,128)S(1)}, f32[512,256]{1,0:T(8,128)S(1)}, f32[512,1]{1,0:T(8,128)S(1)}, bf16[3072,256]{1,0:T(8,128)(2,1)S(1)}, bf16[512,3...) custom-call(f32[256,256]{1,0:T(8,128)} %one_hbm.1, f32[256,256]{1,0:T(8,128)} %two_hbm.1, s32[2,128]{1,0:T(2,128)} %bitcast.1), custom_call_target="tpu_custom_call" | custom-call | tf_op jit(solution)/shard_map/pallas_call | solution.py:335
  30.2 1.6 %shard_map.51 = (f32[256,256]{1,0:T(8,128)}, f32[256,256]{1,0:T(8,128)}) custom-call(f32[512,256]{1,0:T(8,128)S(1)} %get-tuple-element.8.z, f32[512,256]{1,0:T(8,128)S(1)} %get-tuple-element.9.acc, f32[512,1]{1,0:T(8,128)S(1)} %get-tuple-element.10.inv_r, bf16[3072,256]{1,0:T(8,128)(2,1)S(1)} %get-tuple-element.11.k_hi, ...), custom_call_target="tpu_custom_call" | custom-call | tf_op jit(solution)/shard_map/pallas_call | solution.py:380
